TPU v7x, 768 devices: a whole 4x8x12 slice. The times are simulated.
768 devices in a mesh: sec: 192 (over y, z, core), band: 4 (over x).
Axes of the slice: x: 4, y: 8, z: 12, core: 2. Of those that a mesh axis runs over, the one named last changes fastest.
Arguments:
- targets: bfloat16 [2, 160, 192, 4, 512], P(None, None, 'sec', 'band'), may hold values from -36 to 36
- coords: bfloat16 [4, 160, 192, 4, 512], P(None, None, 'sec', 'band'), may hold values from -1 to 1
- pair_first: int32 [192, 4, 512], P('sec', 'band'), may hold values from 1792 to 2815, as said below
- pair_second: int32 [192, 4, 512], P('sec', 'band'), may hold values from 0 to 4607, as said below
- pair_count: int32 [192, 4, 512], P('sec', 'band'), may hold values from 37 to 150, as said below
Outputs:
- solution: float32 [6, 384, 8, 128], P(None, 'sec', 'band')
- next_direction: float32 [6, 384, 8, 128], P(None, 'sec', 'band')
Inputs may be any that keep to these rules, and one draw needn't show every extreme that they name: `pair_first`: for each slab and band the 512 entries name every tile of that slab's and band's own block once, as ((s + 2) * 6 + r + 2) * 128 + c for local section s, row r and column c. `pair_second`: an index of the same form naming a tile of the grid other than the pair's first, at most two sections, two rows and two columns away from it; every other pair lies within one section. `pair_count`: each slab and band has a pair with exactly 150 matches.
All inputs are finite; a program needn't handle non-finite values.
Results may differ from a plain program's by a relative error of at most 0.0012.
Values sent between devices are 32-bit elements; how exact they have to be, the bound alone decides.
A program may use at most 32 MiB of HBM per device.

v0:
```python
import math

import jax
import jax.numpy as jnp
from jax import lax
from jax.sharding import PartitionSpec as P

NCOLS = 128
SEC_DEV = 2
ROWS_DEV = 2


def passed_along(block, axis, distance):
    devices = range(lax.axis_size(axis))
    route = [(i - distance, i) for i in devices if i - distance in devices]
    return lax.ppermute(block, axis, route)


def extended_2(block, sides, width):
    for axis, dim in sides:
        count = lax.axis_size(axis)
        forward = [(i, i + 1) for i in range(count - 1)]
        backward = [(target, source) for source, target in forward]
        low = lax.ppermute(
            lax.slice_in_dim(block, block.shape[dim] - width, None, axis=dim), axis, forward
        )
        high = lax.ppermute(lax.slice_in_dim(block, 0, width, axis=dim), axis, backward)
        block = jnp.concatenate([low, block, high], axis=dim)
    return block


def errors(params, near_index, far_index, points, present):
    near_params = params[:, near_index]
    far_params = params[:, far_index]
    error_x = (
        near_params[0] * points[0]
        + near_params[1] * points[1]
        + near_params[2]
        - (far_params[0] * points[2] + far_params[1] * points[3] + far_params[2])
    )
    error_y = (
        near_params[3] * points[0]
        + near_params[4] * points[1]
        + near_params[5]
        - (far_params[3] * points[2] + far_params[4] * points[3] + far_params[5])
    )
    return (jnp.where(present, error_x, 0.0), jnp.where(present, error_y, 0.0))


def spread(gradient, error_x, error_y, points, near_index, far_index):
    near_terms = jnp.stack(
        [
            jnp.sum(error_x * points[0], axis=0),
            jnp.sum(error_x * points[1], axis=0),
            jnp.sum(error_x, axis=0),
            jnp.sum(error_y * points[0], axis=0),
            jnp.sum(error_y * points[1], axis=0),
            jnp.sum(error_y, axis=0),
        ]
    )
    far_terms = jnp.stack(
        [
            jnp.sum(error_x * points[2], axis=0),
            jnp.sum(error_x * points[3], axis=0),
            jnp.sum(error_x, axis=0),
            jnp.sum(error_y * points[2], axis=0),
            jnp.sum(error_y * points[3], axis=0),
            jnp.sum(error_y, axis=0),
        ]
    )
    return gradient.at[:, near_index].add(near_terms).at[:, far_index].add(-far_terms)


def fold_band(buffer):
    row_count = buffer.shape[2] - 4
    for offset in (1, -1):
        if offset == 1:
            rim_cells = buffer[:, :, row_count + 2 :]
            row_start = 2
        else:
            rim_cells = buffer[:, :, :2]
            row_start = row_count
        received = passed_along(rim_cells, "band", offset)
        buffer = buffer.at[:, :, row_start : row_start + 2].add(received)
    return buffer[:, :, 2 : row_count + 2]


def fold_sec(buffer):
    sec_count = buffer.shape[1] - 4
    for offset in (1, -1):
        if offset == 1:
            rim_cells = buffer[:, sec_count + 2 :]
            sec_start = 2
        else:
            rim_cells = buffer[:, :2]
            sec_start = sec_count
        received = passed_along(rim_cells, "sec", offset)
        buffer = buffer.at[:, sec_start : sec_start + 2].add(received)
    return buffer[:, 2 : sec_count + 2]


def global_sum(value):
    return lax.psum(value, ("sec", "band"))


def on_device(targets, coords, pair_first, pair_second, pair_count):
    slot_count = coords.shape[1]
    pair_total = coords.shape[-1]
    points = coords.reshape(4, slot_count, pair_total).astype(jnp.float32)
    tile_near = pair_first.reshape(pair_total)
    tile_far = pair_second.reshape(pair_total)
    present = lax.broadcasted_iota(jnp.int32, (slot_count, pair_total), 0) < pair_count.reshape(
        1, pair_total
    )
    target = jnp.where(
        present[None], targets.reshape(2, slot_count, pair_total).astype(jnp.float32), 0.0
    )
    wide_shape = (6, SEC_DEV + 4, ROWS_DEV + 4, NCOLS)
    wide_count = (SEC_DEV + 4) * (ROWS_DEV + 4) * NCOLS

    def forward(field):
        extended = extended_2(field, (("sec", 1), ("band", 2)), 2)
        return errors(extended.reshape(6, wide_count), tile_near, tile_far, points, present)

    def adjoint(error_x, error_y):
        buffer = spread(
            jnp.zeros((6, wide_count), jnp.float32), error_x, error_y, points, tile_near, tile_far
        )
        buffer = buffer.reshape(wide_shape)
        return fold_sec(fold_band(buffer))

    beta_one = jnp.sqrt(global_sum(jnp.sum(target * target)))
    t_one = adjoint(target[0] / beta_one, target[1] / beta_one)
    alpha_one = jnp.sqrt(global_sum(jnp.sum(t_one * t_one)))
    v_one = t_one / alpha_one
    image_x, image_y = forward(v_one)
    hat_x = image_x - alpha_one * (target[0] / beta_one)
    hat_y = image_y - alpha_one * (target[1] / beta_one)
    beta_two = jnp.sqrt(global_sum(jnp.sum(hat_x * hat_x) + jnp.sum(hat_y * hat_y)))
    t_two = adjoint(hat_x / beta_two, hat_y / beta_two) - beta_two * v_one
    alpha_two = jnp.sqrt(global_sum(jnp.sum(t_two * t_two)))
    v_two = t_two / alpha_two
    rho_square = alpha_one * alpha_one + beta_two * beta_two
    solution = alpha_one * beta_one / rho_square * v_one
    tile_all = 6 * SEC_DEV * ROWS_DEV * NCOLS * lax.axis_size("sec") * lax.axis_size("band")
    direction = math.sqrt(float(tile_all)) * (v_two - beta_two * alpha_two / rho_square * v_one)
    return (solution, direction)


def solution(mesh):
    return jax.shard_map(
        on_device,
        mesh=mesh,
        in_specs=(
            P(None, None, "sec", "band", None),
            P(None, None, "sec", "band", None),
            P("sec", "band", None),
            P("sec", "band", None),
            P("sec", "band", None),
        ),
        out_specs=(P(None, "sec", "band", None), P(None, "sec", "band", None)),
        check_vma=False,
    )
```

profile of v0, /device:TPU:1, one launch (start us, length us, event | category | flops | bytes accessed | tf_op | source)
XLA Modules:
  0.0 547.4 jit_solution(3693404347800868272)
XLA Ops:
  1.4 1.8 convert_select_fusion
  3.1 120.4 %psum.28 = f32[]{:T(128)} all-reduce(f32[]{:T(128)} %get-tuple-element.147), channel_id=1, replica_groups=mesh['sec'=192,'band'=4] {'sec','band'}, use_global_device_ids=true, to_apply=%region_1.2 | all-reduce | flops 1 | bytes 8 | tf_op jit(solution)/shard_map/psum | solution.py:103
  126.3 3.8 scatter_custom_fusion
  130.1 6.1 %scatter_fusion = f32[6,4608]{0,1:T(8,128)} fusion(f32[6,4608]{0,1:T(8,128)} %scatter_custom_fusion, s32[512]{0:T(512)S(1)} %bitcast.151, f32[512,6]{1,0:T(8,128)S(1)} %copy.17), kind=kCustom, calls=%fused_computation.3 | custom fusion | flops 3072 | bytes 38912 | tf_op jit(solution)/shard_map/scatter-add | solution.py:71
  136.2 2.7 fusion.26
  138.9 2.0 copy.28
  140.9 3.0 collective-permute-start
  146.3 3.3 collective-permute-done.1
  150.5 4.2 collective-permute-start.2
  154.7 1.9 collective-permute-start.3
  156.6 3.1 collective-permute-done.3
  160.3 105.1 %psum.29 = f32[]{:T(128)} all-reduce(f32[]{:T(128)} %multiply_reduce_fusion.12), channel_id=1, replica_groups=mesh['sec'=192,'band'=4] {'sec','band'}, use_global_device_ids=true, to_apply=%region_15.16 | all-reduce | flops 1 | bytes 8 | tf_op jit(solution)/shard_map/psum | solution.py:103
  266.1 2.6 collective-permute-start.4
  268.7 1.9 collective-permute-start.5
  270.7 3.1 collective-permute-done.5
  273.8 3.7 collective-permute-start.6
  278.7 3.4 collective-permute-done.7
  282.2 2.1 copy.21
  284.3 2.7 gather_fusion
  287.0 2.7 gather_fusion.1
  289.7 1.6 slice_reduce_fusion.2
  294.3 109.9 %psum.30 = f32[]{:T(128)} all-reduce(f32[]{:T(128)S(6)} %add.176), channel_id=1, replica_groups=mesh['sec'=192,'band'=4] {'sec','band'}, use_global_device_ids=true, to_apply=%region_18.19 | all-reduce | flops 1 | bytes 8 | tf_op jit(solution)/shard_map/psum | solution.py:103
  405.5 2.8 scatter_custom_fusion.2
  408.3 4.2 scatter_fusion.1
  413.9 1.4 copy.31
  415.2 3.7 collective-permute-start.8
  418.9 1.4 copy.32
  421.9 3.1 collective-permute-done.9
  425.1 3.6 collective-permute-start.10
  428.7 1.9 collective-permute-start.11
  430.7 3.0 collective-permute-done.11
  434.3 111.8 %psum.31 = f32[]{:T(128)} all-reduce(f32[]{:T(128)} %get-tuple-element.134), channel_id=1, replica_groups=mesh['sec'=192,'band'=4] {'sec','band'}, use_global_device_ids=true, to_apply=%region_32.33 | all-reduce | flops 1 | bytes 8 | tf_op jit(solution)/shard_map/psum | solution.py:103
  (50 shorter events, 14.4 us)
Async XLA Ops:
  124.3 1.8 copy-start.1
  124.3 2.1 copy-start.2
  140.9 5.5 collective-permute-start
  144.8 4.9 collective-permute-start.1
  150.5 6.1 %collective-permute-start.2 = (f32[6,2,2,128]{3,2,1,0:T(2,128)S(1)}, f32[6,2,2,128]{3,2,1,0:T(2,128)S(1)}, u32[]{:S(2)}, u32[]{:S(2)}) collective-permute-start(f32[6,2,2,128]{3,2,1,0:T(2,128)S(1)} %get-tuple-element.150), channel_id=1, source_target_pairs={{0,4},{4,8},{8,12},{12,16},{16,20},{20,24},{24,28},{28,32},{32,36}... | collective-permute-start | bytes 36872 | tf_op jit(solution)/shard_map/ppermute | solution.py:16
  154.7 5.0 collective-permute-start.3
  266.1 4.6 collective-permute-start.4
  268.7 5.0 collective-permute-start.5
  273.8 5.0 collective-permute-start.6
  277.4 4.7 collective-permute-start.7
  284.3 7.0 %copy-start = (s32[1,1,512]{2,1,0:T(1,128)S(1)}, s32[1,1,512]{2,1,0:T(1,128)}, u32[]{:S(2)}) copy-start(s32[1,1,512]{2,1,0:T(1,128)} %param.25) | copy-start | bytes 6148
  415.2 6.6 %collective-permute-start.8 = (f32[6,6,2,128]{3,2,1,0:T(2,128)S(1)}, f32[6,6,2,128]{3,2,1,0:T(2,128)S(1)}, u32[]{:S(2)}, u32[]{:S(2)}) collective-permute-start(f32[6,6,2,128]{3,2,1,0:T(2,128)S(1)} %copy.31), channel_id=1, source_target_pairs={{0,1},{1,2},{2,3},{4,5},{5,6},{6,7},{8,9},{9,10},{10,11},{12,13},{... | collective-permute-start | bytes 110600 | tf_op jit(solution)/shard_map/ppermute | solution.py:16
  420.3 4.7 collective-permute-start.9
  425.1 5.6 %collective-permute-start.10 = (f32[6,2,2,128]{3,2,1,0:T(2,128)S(1)}, f32[6,2,2,128]{3,2,1,0:T(2,128)S(1)}, u32[]{:S(2)}, u32[]{:S(2)}) collective-permute-start(f32[6,2,2,128]{3,2,1,0:T(2,128)S(1)} %get-tuple-element.148), channel_id=1, source_target_pairs={{0,4},{4,8},{8,12},{12,16},{16,20},{20,24},{24,28},{28,32},{32,36}... | collective-permute-start | bytes 36872 | tf_op jit(solution)/shard_map/ppermute | solution.py:16
  428.7 5.0 collective-permute-start.11
where the time goes:
time: 554 us; the launch traced here: 547 us
  blocking collectives  447 us (81%)
  starting transfers between devices  30.3 us (5%)
  other arithmetic  25.6 us (5%)
  local copies, waits for them, and re-layouts  20.1 us (4%)
  waiting for transfers between devices  19 us (3%)
    psum x4, blocking collectives, global_sum(): return lax.psum(value, ('sec', 'band'))  447 us
    ppermute x8, starting transfers between devices, passed_along(): return lax.ppermute(block, axis, route)  20.9 us
    scatter-add x4, other arithmetic, spread(): gradient.at[:, near_index].add(near_terms).at[:, far_index].add(-far_terms)  16.8 us
    ppermute x8, waiting for transfers between devices, passed_along(): return lax.ppermute(block, axis, route)  12.6 us
  transfers between devices with their start and end apart: 12, of which 6 were waited for; matrix products, arithmetic and copies ran while one was open for 1% of the time, Pallas kernels for 0%

commit v1 on v0

v1 whole, which is shorter than its diff:
```python
import functools
import math

import jax
import jax.numpy as jnp
from jax import lax
from jax.experimental import pallas as pl
from jax.experimental.pallas import tpu as pltpu
from jax.sharding import PartitionSpec as P

NCOLS = 128
SEC_DEV = 2
ROWS_DEV = 2
TILE_ROWS = SEC_DEV * ROWS_DEV
ROWS_WIDE = ROWS_DEV + 4
MESH = pl.DeviceIdType.MESH
F32 = jnp.float32
SHIFTS = (-2, -1, 0, 1, 2)
NEIGHBOURS = tuple((a, b) for a in (-1, 0, 1) for b in (-1, 0, 1) if (a, b) != (0, 0))

SUMS = (
    "xp",
    "yp",
    "xq",
    "yq",
    "xpxp",
    "xpyp",
    "ypyp",
    "xqxq",
    "xqyq",
    "yqyq",
    "xpxq",
    "xpyq",
    "ypxq",
    "ypyq",
    "rx",
    "ry",
    "rxxp",
    "rxyp",
    "ryxp",
    "ryyp",
    "rxxq",
    "rxyq",
    "ryxq",
    "ryyq",
)
GROUPS = (
    ("-rxxq", "-rxyq", "-rx", "code", "-ryxq", "-ryyq", "-ry", "0"),
    ("xpxq", "xpyq", "xp", "0", "ypxq", "ypyq", "yp", "0"),
    ("xq", "yq", "n", "0", "xqxq", "xqyq", "yqyq", "0"),
    ("rxxp", "rxyp", "rx", "0", "ryxp", "ryyp", "ry", "0"),
    ("xp", "yp", "n", "0", "xpxp", "xpyp", "ypyp", "0"),
    ("xpxq", "ypxq", "xq", "0", "xpyq", "ypyq", "yq", "0"),
)
TABLE = tuple(name for group in GROUPS for name in group)


def halves(block):
    turned = pltpu.roll(block, 4, 0)
    upper = lax.broadcasted_iota(jnp.int32, (8, NCOLS), 0) < 4
    return jnp.where(upper, block, turned), jnp.where(upper, turned, block)


def row_of(block, upper_row, lower_row):
    upper = lax.broadcasted_iota(jnp.int32, (8, NCOLS), 0) < 4
    one = jnp.broadcast_to(block[upper_row : upper_row + 1], (8, NCOLS))
    two = jnp.broadcast_to(block[lower_row : lower_row + 1], (8, NCOLS))
    return jnp.where(upper, one, two)


def pair_tables(coords_ref, targets_ref, first_ref, second_ref, count_ref, table):
    slots = coords_ref.shape[1]
    pairs = coords_ref.shape[2]
    first = first_ref[...]
    second = second_ref[...]

    def place(index):
        row = lax.shift_right_logical(index, 7)
        section = lax.shift_right_logical(row * 43, 8)
        return section, row - section * ROWS_WIDE, lax.bitwise_and(index, NCOLS - 1)

    near, far = place(first), place(second)
    code = ((far[0] - near[0]) * 16 + far[1] - near[1]) * 16 + far[2] - near[2]
    lines = {"code": code.astype(F32), "n": count_ref[...].astype(F32)}
    squares = jnp.zeros((8, NCOLS), F32)
    for block in range(pairs // NCOLS):
        lanes = pl.ds(block * NCOLS, NCOLS)
        count = jnp.broadcast_to(count_ref[:, lanes], (16, NCOLS))

        def chunk(k, sums):
            rows = pl.ds(pl.multiple_of(k * 16, 16), 16)
            present = lax.broadcasted_iota(jnp.int32, (16, NCOLS), 0) + k * 16 < count

            def load(ref, i):
                return jnp.where(present, ref[i, rows, lanes].astype(F32), 0.0)

            v = {"xp": load(coords_ref, 0), "yp": load(coords_ref, 1), "xq": load(coords_ref, 2)}
            v.update(yq=load(coords_ref, 3), rx=load(targets_ref, 0), ry=load(targets_ref, 1))
            out = []
            for name, total in zip(SUMS, sums):
                term = v[name] if len(name) == 2 else v[name[:2]] * v[name[2:]]
                out.append(total + (term[:8] + term[8:]))
            square = v["rx"] * v["rx"] + v["ry"] * v["ry"]
            out.append(sums[-1] + (square[:8] + square[8:]))
            return tuple(out)

        zero = jnp.zeros((8, NCOLS), F32)
        sums = lax.fori_loop(0, slots // 16, chunk, (zero,) * len(SUMS) + (squares,))
        squares = sums[-1]
        totals = {name: jnp.sum(s, axis=0, keepdims=True) for name, s in zip(SUMS, sums)}
        for row, name in enumerate(TABLE):
            if name == "0":
                line = jnp.zeros((1, NCOLS), F32)
            elif name in lines:
                line = lines[name][:, block * NCOLS : (block + 1) * NCOLS]
            elif name[0] == "-":
                line = -totals[name[1:]]
            else:
                line = totals[name]
            table[row : row + 1, lanes] = line
    return squares


def by_first_tile(first_ref, table, store):
    values = table[...]
    high = values.astype(jnp.bfloat16)
    rest = values - high.astype(F32)
    middle = rest.astype(jnp.bfloat16)
    low = (rest - middle.astype(F32)).astype(jnp.bfloat16)
    parts = jnp.concatenate([high, middle, low], axis=0)
    height, pairs = values.shape
    first = jnp.broadcast_to(first_ref[...], (NCOLS, pairs))
    column = lax.broadcasted_iota(jnp.int32, (NCOLS, pairs), 0)
    for tile_row in range(TILE_ROWS):
        start = ((tile_row // ROWS_DEV + 2) * ROWS_WIDE + tile_row % ROWS_DEV + 2) * NCOLS
        chosen = jnp.where(first == column + start, 1.0, 0.0).astype(jnp.bfloat16)
        moved = lax.dot_general(
            parts, chosen, (((1,), (1,)), ((), ())), preferred_element_type=F32
        )
        moved = moved[:height] + moved[height : 2 * height] + moved[2 * height :]
        for group in range(len(GROUPS)):
            store(group, tile_row, moved[8 * group : 8 * group + 8])


def origin(source):
    block, row = source // TILE_ROWS, lax.rem(source, TILE_ROWS)
    section = (block // 3 - 1) * SEC_DEV + row // ROWS_DEV
    return (section * 256 + (lax.rem(block, 3) - 1) * (ROWS_DEV * 16) + lax.rem(row, ROWS_DEV) * 16)


def target_key(tile_row):
    return float(tile_row // ROWS_DEV * 256 + tile_row % ROWS_DEV * 16)


def kernel(
    sections,
    bands,
    group_one,
    coords_ref,
    targets_ref,
    first_ref,
    second_ref,
    count_ref,
    solution_ref,
    direction_ref,
    table,
    terms,
    moments,
    local,
    keys,
    field,
    sums_one,
    sums_two,
    terms_send,
    terms_recv,
    moments_send,
    moments_recv,
    field_send,
    field_recv,
    sums_send,
    sums_recv,
):
    sec = lax.axis_index("sec")
    band = lax.axis_index("band")
    group_two = sections // group_one * bands

    def neighbour(a, b):
        return (lax.rem(sec + a + sections, sections), lax.rem(band + b + bands, bands))

    def peer_one(d):
        base = sec // group_one * group_one
        return (base + lax.rem(lax.rem(sec, group_one) + d, group_one), band)

    def peer_two(d):
        i = lax.rem(sec // group_one * bands + band + d, group_two)
        return (i // bands * group_one + lax.rem(sec, group_one), lax.rem(i, bands))

    barrier = pltpu.get_barrier_semaphore()
    for a, b in NEIGHBOURS:
        pl.semaphore_signal(barrier, inc=1, device_id=neighbour(a, b), device_id_type=MESH)

    def greet(peer, d, carry):
        pl.semaphore_signal(barrier, inc=1, device_id=peer(d), device_id_type=MESH)
        return carry

    lax.fori_loop(1, group_one, functools.partial(greet, peer_one), 0)
    lax.fori_loop(1, group_two, functools.partial(greet, peer_two), 0)

    squares = pair_tables(coords_ref, targets_ref, first_ref, second_ref, count_ref, table)

    def store(group, tile_row, value):
        if group == 0:
            terms[4, tile_row] = value
        elif group < 3:
            moments[4, group - 1, tile_row] = value
        else:
            local[group - 3, tile_row] = value

    by_first_tile(first_ref, table, store)

    pl.semaphore_wait(barrier, 8 + group_one - 1 + group_two - 1)

    def exchange(buffer, send, recv):
        copies = []
        for i, (a, b) in enumerate(NEIGHBOURS):
            copies.append(
                pltpu.make_async_remote_copy(
                    src_ref=buffer.at[4],
                    dst_ref=buffer.at[(1 - a) * 3 + 1 - b],
                    send_sem=send.at[i],
                    recv_sem=recv.at[i],
                    device_id=neighbour(a, b),
                    device_id_type=MESH,
                )
            )
            copies[-1].start()
        return copies

    terms_copies = exchange(terms, terms_send, terms_recv)
    moments_copies = exchange(moments, moments_send, moments_recv)
    for copy in terms_copies:
        copy.wait_recv()

    zero = jnp.zeros((8, NCOLS), F32)

    def add_terms(source, totals):
        totals = list(totals)
        block, row = source // TILE_ROWS, lax.rem(source, TILE_ROWS)
        value = terms[block, row]
        place = jnp.broadcast_to(value[3:4], (8, NCOLS)) + origin(source).astype(F32)
        for i, shift in enumerate(SHIFTS):
            moved = pltpu.roll(value, shift % NCOLS, 1)
            key = pltpu.roll(place, shift % NCOLS, 1) - float(shift)
            keys[source, i] = key
            for t in range(TILE_ROWS):
                totals[t] = totals[t] + jnp.where(key == target_key(t), moved, 0.0)
        return tuple(totals)

    totals = lax.fori_loop(0, 9 * TILE_ROWS, add_terms, (zero,) * TILE_ROWS)
    held = lax.rem(lax.broadcasted_iota(jnp.int32, (8, NCOLS), 0), 4) < 3
    gradient = []
    for t in range(TILE_ROWS):
        gradient.append(jnp.where(held, totals[t] + local[0, t], 0.0))
        field[4, t] = gradient[t]
    field_copies = exchange(field, field_send, field_recv)

    for copy in moments_copies:
        copy.wait_recv()

    def add_blocks(source, totals):
        totals = list(totals)
        block, row = source // TILE_ROWS, lax.rem(source, TILE_ROWS)
        value = moments[block, 1, row]
        for i, shift in enumerate(SHIFTS):
            moved = pltpu.roll(value, shift % NCOLS, 1)
            key = keys[source, i]
            for t in range(TILE_ROWS):
                totals[t] = totals[t] + jnp.where(key == target_key(t), moved, 0.0)
        return tuple(totals)

    blocks = lax.fori_loop(0, 9 * TILE_ROWS, add_blocks, (zero,) * TILE_ROWS)
    gg = zero
    own = []
    for t in range(TILE_ROWS):
        g = gradient[t]
        gg = gg + g * g
        upper, lower = halves(blocks[t] + local[1, t])
        line = lax.rem(lax.broadcasted_iota(jnp.int32, (8, NCOLS), 0), 4)
        xx, xy, yy = (row_of(lower, k, k) for k in range(3))
        x, y = (row_of(upper, k, k) for k in range(2))
        first = jnp.where(line == 0, xx, jnp.where(line == 1, xy, jnp.where(line == 2, x, 0.0)))
        second = jnp.where(line == 0, xy, jnp.where(line == 1, yy, jnp.where(line == 2, y, 0.0)))
        own.append(first * row_of(g, 0, 4) + second * row_of(g, 1, 5) + upper * row_of(g, 2, 6))

    for copy in field_copies:
        copy.wait_recv()

    def apply(source, carry):
        far, totals = list(carry[:20]), list(carry[20:])
        block, row = source // TILE_ROWS, lax.rem(source, TILE_ROWS)
        g = field[block, row]
        here = origin(source).astype(F32)
        for t in range(TILE_ROWS):
            for i in range(5):
                far[t * 5 + i] = jnp.where(keys[16 + t, i] == here, g, far[t * 5 + i])
        by_a, by_b = halves(moments[block, 0, row])
        by_c, _ = halves(moments[block, 1, row])
        value = by_a * row_of(g, 0, 4) + by_b * row_of(g, 1, 5) + by_c * row_of(g, 2, 6)
        for i, shift in enumerate(SHIFTS):
            moved = pltpu.roll(value, shift % NCOLS, 1)
            key = keys[source, i]
            for t in range(TILE_ROWS):
                totals[t] = totals[t] + jnp.where(key == target_key(t), moved, 0.0)
        return tuple(far) + tuple(totals)

    carry = lax.fori_loop(0, 9 * TILE_ROWS, apply, (zero,) * 24)
    wg, ww = zero, zero
    product = []
    for t in range(TILE_ROWS):
        far = carry[t * 5 + 2]
        for i, shift in enumerate(SHIFTS):
            if shift:
                far = far + pltpu.roll(carry[t * 5 + i], -shift % NCOLS, 1)
        by_a, by_b = halves(local[2, t])
        by_c, _ = halves(local[1, t])
        near = by_a * row_of(far, 0, 4) + by_b * row_of(far, 1, 5) + by_c * row_of(far, 2, 6)
        w = jnp.where(held, own[t] - near - carry[20 + t], 0.0)
        product.append(w)
        wg = wg + w * gradient[t]
        ww = ww + w * w

    lane = lax.broadcasted_iota(jnp.int32, (1, NCOLS), 1)
    line = jnp.zeros((1, NCOLS), F32)
    for k, part in enumerate((squares, gg, wg, ww)):
        total = jnp.sum(jnp.sum(part, axis=0, keepdims=True), axis=1, keepdims=True)
        line = jnp.where(lane == k, total, line)

    def spread_sum(line, buffer, count, peer, i):
        buffer[0:1, :] = line

        def send(d, carry):
            pltpu.make_async_remote_copy(
                src_ref=buffer.at[pl.ds(0, 1), :],
                dst_ref=buffer.at[pl.ds(d, 1), :],
                send_sem=sums_send.at[i],
                recv_sem=sums_recv.at[i],
                device_id=peer(d),
                device_id_type=MESH,
            ).start()
            return carry

        lax.fori_loop(1, count, send, 0)
        others = buffer.at[pl.ds(1, count - 1), :]
        pltpu.make_async_copy(others, others, sums_recv.at[i]).wait()
        return jnp.sum(buffer[0:count, :], axis=0, keepdims=True)

    line = spread_sum(line, sums_one, group_one, peer_one, 0)
    line = spread_sum(line, sums_two, group_two, peer_two, 1)

    def total_of(k):
        return jnp.sum(jnp.where(lane == k, line, 0.0), axis=1, keepdims=True)

    rr, gg, wg, ww = (total_of(k) for k in range(4))
    beta_one = jnp.sqrt(rr)
    norm_g = jnp.sqrt(gg)
    alpha_one = norm_g / beta_one
    beta_two_sq = wg / gg - alpha_one * alpha_one
    beta_two = jnp.sqrt(beta_two_sq)
    on_w = 1.0 / (norm_g * beta_two)
    on_g = -(alpha_one / (beta_one * beta_two) + beta_two / norm_g)
    scaled = on_g / on_w
    alpha_two = on_w * jnp.sqrt(ww + scaled * (2.0 * wg + scaled * gg))
    rho_sq = alpha_one * alpha_one + beta_two_sq
    first_scale = alpha_one * beta_one / (rho_sq * norm_g)
    root = math.sqrt(float(6 * TILE_ROWS * NCOLS * sections * bands))
    scale_w = root * on_w / alpha_two
    scale_g = root * (on_g / alpha_two - beta_two * alpha_two / (rho_sq * norm_g))
    for t in range(TILE_ROWS):
        one = first_scale * gradient[t]
        two = scale_w * product[t] + scale_g * gradient[t]
        for k, row in enumerate((0, 1, 2, 4, 5, 6)):
            solution_ref[k, t : t + 1, :] = one[row : row + 1]
            direction_ref[k, t : t + 1, :] = two[row : row + 1]

    for copies in (terms_copies, moments_copies, field_copies):
        for copy in copies:
            copy.wait_send()
    for buffer, count, i in ((sums_one, group_one, 0), (sums_two, group_two, 1)):
        others = buffer.at[pl.ds(1, count - 1), :]
        pltpu.make_async_copy(others, others, sums_send.at[i]).wait()


def solution(mesh):
    sections, bands = mesh.shape["sec"], mesh.shape["band"]
    group_one = 24 if sections % 24 == 0 else 2
    group_two = sections // group_one * bands

    def on_device(targets, coords, pair_first, pair_second, pair_count):
        slots, pairs = coords.shape[1], coords.shape[-1]
        vmem = pl.BlockSpec(memory_space=pltpu.VMEM)
        shape = (6, TILE_ROWS, NCOLS)
        tile = (8, NCOLS)
        dma = pltpu.SemaphoreType.DMA
        outputs = pl.pallas_call(
            functools.partial(kernel, sections, bands, group_one),
            out_shape=(jax.ShapeDtypeStruct(shape, F32), jax.ShapeDtypeStruct(shape, F32)),
            in_specs=[vmem] * 5,
            out_specs=(vmem, vmem),
            scratch_shapes=[
                pltpu.VMEM((8 * len(GROUPS), pairs), F32),
                pltpu.VMEM((9, TILE_ROWS) + tile, F32),
                pltpu.VMEM((9, 2, TILE_ROWS) + tile, F32),
                pltpu.VMEM((3, TILE_ROWS) + tile, F32),
                pltpu.VMEM((9 * TILE_ROWS, 5) + tile, F32),
                pltpu.VMEM((9, TILE_ROWS) + tile, F32),
                pltpu.VMEM((group_one, NCOLS), F32),
                pltpu.VMEM((group_two, NCOLS), F32),
            ]
            + [dma((8,))] * 6
            + [dma((2,))] * 2,
            compiler_params=pltpu.CompilerParams(
                collective_id=0, has_side_effects=True, vmem_limit_bytes=32 * 2**20
            ),
        )(
            coords.reshape(4, slots, pairs),
            targets.reshape(2, slots, pairs),
            pair_first.reshape(1, pairs),
            pair_second.reshape(1, pairs),
            pair_count.reshape(1, pairs),
        )
        return tuple(o.reshape(6, SEC_DEV, ROWS_DEV, NCOLS) for o in outputs)

    return jax.shard_map(
        on_device,
        mesh=mesh,
        in_specs=(
            P(None, None, "sec", "band", None),
            P(None, None, "sec", "band", None),
            P("sec", "band", None),
            P("sec", "band", None),
            P("sec", "band", None),
        ),
        out_specs=(P(None, "sec", "band", None), P(None, "sec", "band", None)),
        check_vma=False,
    )
```

time: 554 us -> 51.3 us (0.09); the launches traced: 547 us -> 51.1 us
  blocking collectives: 447 us -> 0 us
  Pallas kernels: 0 us -> 46.4 us
  starting transfers between devices: 30.3 us -> 0 us
  other arithmetic: 25.6 us -> 0 us
  waiting for transfers between devices: 19 us -> 0 us
  local copies, waits for them, and re-layouts: 20.1 us -> 3.95 us
    psum x4 -> x0, blocking collectives: 447 us -> none  [global_sum(): return lax.psum(value, ('sec', 'band'))]
    pallas_call x0 -> x1, Pallas kernels: none -> 46.4 us  [on_device(): pl.pallas_call(functools.partial(kernel, sections, bands, group_one), out...]
    ppermute x12 -> x0, starting transfers between devices: 30.3 us -> none  [the longest x8 20.9 us: passed_along(): return lax.ppermute(block, axis, route)]
    ppermute x12 -> x0, waiting for transfers between devices: 19 us -> none  [the longest x8 12.6 us: passed_along(): return lax.ppermute(block, axis, route)]
    scatter-add x4 -> x0, other arithmetic: 16.8 us -> none  [spread(): gradient.at[:, near_index].add(near_terms).at[:, far_index].add(-far_terms)]
    slice x5 -> x0, local copies, waits for them, and re-layouts: 5.65 us -> none  [the longest x2 4.04 us: fold_band(): rim_cells = buffer[:, :, row_count + 2:]]
  transfers between devices with their start and end apart: 12 -> 0, of which waited for: 6 -> 0; matrix products, arithmetic and copies ran while one was open for 1% -> 0% of each run, Pallas kernels for 0% -> 0%
where the time goes in v1:
time: 51.3 us; the launch traced here: 51.1 us
  Pallas kernels  46.4 us (90%)
  local copies, waits for them, and re-layouts  3.95 us (8%)
  between operations  0.67 us (1%)
    pallas_call x1, Pallas kernels, on_device(): pl.pallas_call(functools.partial(kernel, sections, bands, group_one), out...  46.4 us
    unnamed x12, local copies, waits for them, and re-layouts  3.95 us

profile of v1, /device:TPU:1, one launch (start us, length us, event | category | flops | bytes accessed | tf_op | source)
XLA Modules:
  0.0 51.1 jit_solution(10025129586867895573)
XLA Ops:
  0.6 0.0 copy-start.4
  0.6 0.0 copy-start.3
  0.7 0.0 copy-start.2
  0.7 0.7 %copy-done.4 = s32[1,1,512]{2,1,0:T(1,128)S(1)} copy-done((s32[1,1,512]{2,1,0:T(1,128)S(1)}, s32[1,1,512]{2,1,0:T(1,128)}, u32[]{:S(2)}) %copy-start.4) | copy-done | bytes 2072
  1.3 0.0 copy-done.3
  1.3 0.0 copy-done.2
  1.3 0.0 copy-start
  1.3 1.1 %copy-done = bf16[4,160,1,1,512]{4,1,3,2,0:T(8,128)(2,1)S(1)} copy-done((bf16[4,160,1,1,512]{4,1,3,2,0:T(8,128)(2,1)S(1)}, bf16[4,160,1,1,512]{4,1,3,2,0:T(8,128)(2,1)}, u32[]{:S(2)}) %copy-start) | copy-done | bytes 655384
  2.4 0.0 copy-start.1
  2.4 1.0 %copy-done.1 = bf16[2,160,1,1,512]{4,1,3,2,0:T(8,128)(2,1)S(1)} copy-done((bf16[2,160,1,1,512]{4,1,3,2,0:T(8,128)(2,1)S(1)}, bf16[2,160,1,1,512]{4,1,3,2,0:T(8,128)(2,1)}, u32[]{:S(2)}) %copy-start.1) | copy-done | bytes 327704
  3.4 46.4 %shard_map.68 = (f32[6,4,128]{2,1,0:T(4,128)S(1)}, f32[6,4,128]{2,1,0:T(4,128)S(1)}) custom-call(bf16[4,160,512]{2,1,0:T(8,128)(2,1)S(1)} %bitcast.7, bf16[2,160,512]{2,1,0:T(8,128)(2,1)S(1)} %bitcast.8, s32[1,512]{1,0:T(1,128)S(1)} %bitcast.11, s32[1,512]{1,0:T(1,128)S(1)} %bitcast.12, s32[1,512]{1,0:T(1,128)S(1)} %bitcast.13), custom_call_target="tpu_custom_call" | custom-call | tf_op jit(solution)/shard_map/pallas_call | solution.py:404
  49.9 0.6 %copy.9 = f32[6,2,2,128]{3,2,1,0:T(2,128)} copy(f32[6,2,2,128]{3,2,1,0:T(2,128)S(1)} %bitcast.10) | data formatting | bytes 24576
  50.5 0.6 %copy.10 = f32[6,2,2,128]{3,2,1,0:T(2,128)} copy(f32[6,2,2,128]{3,2,1,0:T(2,128)S(1)} %bitcast.9) | data formatting | bytes 24576
Async XLA Ops:
  0.6 0.7 %copy-start.4 = (s32[1,1,512]{2,1,0:T(1,128)S(1)}, s32[1,1,512]{2,1,0:T(1,128)}, u32[]{:S(2)}) copy-start(s32[1,1,512]{2,1,0:T(1,128)} %param.9) | copy-start | bytes 6148
  0.6 0.7 %copy-start.3 = (s32[1,1,512]{2,1,0:T(1,128)S(1)}, s32[1,1,512]{2,1,0:T(1,128)}, u32[]{:S(2)}) copy-start(s32[1,1,512]{2,1,0:T(1,128)} %param.8) | copy-start | bytes 6148
  0.7 0.7 %copy-start.2 = (s32[1,1,512]{2,1,0:T(1,128)S(1)}, s32[1,1,512]{2,1,0:T(1,128)}, u32[]{:S(2)}) copy-start(s32[1,1,512]{2,1,0:T(1,128)} %param.7) | copy-start | bytes 6148
  1.3 1.1 %copy-start = (bf16[4,160,1,1,512]{4,1,3,2,0:T(8,128)(2,1)S(1)}, bf16[4,160,1,1,512]{4,1,3,2,0:T(8,128)(2,1)}, u32[]{:S(2)}) copy-start(bf16[4,160,1,1,512]{4,1,3,2,0:T(8,128)(2,1)} %param.6) | copy-start | bytes 1966084
  2.4 1.0 %copy-start.1 = (bf16[2,160,1,1,512]{4,1,3,2,0:T(8,128)(2,1)S(1)}, bf16[2,160,1,1,512]{4,1,3,2,0:T(8,128)(2,1)}, u32[]{:S(2)}) copy-start(bf16[2,160,1,1,512]{4,1,3,2,0:T(8,128)(2,1)} %param.5) | copy-start | bytes 983044

commit v2 on v1

--- a/solution.py
+++ b/solution.py
@@ -14,9 +14,10 @@
 TILE_ROWS = SEC_DEV * ROWS_DEV
 ROWS_WIDE = ROWS_DEV + 4
 MESH = pl.DeviceIdType.MESH
+CHUNKS = 5
 F32 = jnp.float32
 SHIFTS = (-2, -1, 0, 1, 2)
-NEIGHBOURS = tuple((a, b) for a in (-1, 0, 1) for b in (-1, 0, 1) if (a, b) != (0, 0))
+NEIGHBOURS = ((-1, -1), (1, -1), (-1, 1), (1, 1), (-1, 0), (1, 0), (0, -1), (0, 1))
 
 SUMS = (
     "xp",
@@ -45,30 +46,29 @@
     "ryyq",
 )
 GROUPS = (
-    ("-rxxq", "-rxyq", "-rx", "code", "-ryxq", "-ryyq", "-ry", "0"),
-    ("xpxq", "xpyq", "xp", "0", "ypxq", "ypyq", "yp", "0"),
-    ("xq", "yq", "n", "0", "xqxq", "xqyq", "yqyq", "0"),
-    ("rxxp", "rxyp", "rx", "0", "ryxp", "ryyp", "ry", "0"),
-    ("xp", "yp", "n", "0", "xpxp", "xpyp", "ypyp", "0"),
-    ("xpxq", "ypxq", "xq", "0", "xpyq", "ypyq", "yq", "0"),
+    ("-rxxq", "-rxyq", "-rx", "-ryxq", "-ryyq", "-ry", "0", "0"),
+    ("xpxq", "xpyq", "xp", "ypxq", "ypyq", "yp", "code", "0"),
+    ("xq", "yq", "n", "xqxq", "xqyq", "yqyq", "0", "0"),
+    ("rxxp", "rxyp", "rx", "ryxp", "ryyp", "ry", "0", "0"),
+    ("xp", "yp", "n", "xpxp", "xpyp", "ypyp", "0", "0"),
+    ("xpxq", "ypxq", "xq", "xpyq", "ypyq", "yq", "0", "0"),
 )
 TABLE = tuple(name for group in GROUPS for name in group)
 
 
 def halves(block):
-    turned = pltpu.roll(block, 4, 0)
-    upper = lax.broadcasted_iota(jnp.int32, (8, NCOLS), 0) < 4
-    return jnp.where(upper, block, turned), jnp.where(upper, turned, block)
+    upper = lax.broadcasted_iota(jnp.int32, (8, NCOLS), 0) < 3
+    return jnp.where(upper, block, pltpu.roll(block, 3, 0)), jnp.where(upper, pltpu.roll(block, 5, 0), block)
 
 
 def row_of(block, upper_row, lower_row):
-    upper = lax.broadcasted_iota(jnp.int32, (8, NCOLS), 0) < 4
+    upper = lax.broadcasted_iota(jnp.int32, (8, NCOLS), 0) < 3
     one = jnp.broadcast_to(block[upper_row : upper_row + 1], (8, NCOLS))
     two = jnp.broadcast_to(block[lower_row : lower_row + 1], (8, NCOLS))
     return jnp.where(upper, one, two)
 
 
-def pair_tables(coords_ref, targets_ref, first_ref, second_ref, count_ref, table):
+def pair_tables(coords_ref, targets_ref, first_ref, second_ref, count_ref, table, ready):
     slots = coords_ref.shape[1]
     pairs = coords_ref.shape[2]
     first = first_ref[...]
@@ -86,6 +86,7 @@
     for block in range(pairs // NCOLS):
         lanes = pl.ds(block * NCOLS, NCOLS)
         count = jnp.broadcast_to(count_ref[:, lanes], (16, NCOLS))
+        ready(block)
 
         def chunk(k, sums):
             rows = pl.ds(pl.multiple_of(k * 16, 16), 16)
@@ -104,8 +105,14 @@
             out.append(sums[-1] + (square[:8] + square[8:]))
             return tuple(out)
 
+        def chunks(k, sums):
+            for i in range(CHUNKS):
+                sums = chunk(k * CHUNKS + i, sums)
+            return sums
+
         zero = jnp.zeros((8, NCOLS), F32)
-        sums = lax.fori_loop(0, slots // 16, chunk, (zero,) * len(SUMS) + (squares,))
+        sums = (zero,) * len(SUMS) + (squares,)
+        sums = lax.fori_loop(0, slots // (16 * CHUNKS), chunks, sums)
         squares = sums[-1]
         totals = {name: jnp.sum(s, axis=0, keepdims=True) for name, s in zip(SUMS, sums)}
         for row, name in enumerate(TABLE):
@@ -142,14 +149,107 @@
             store(group, tile_row, moved[8 * group : 8 * group + 8])
 
 
-def origin(source):
-    block, row = source // TILE_ROWS, lax.rem(source, TILE_ROWS)
-    section = (block // 3 - 1) * SEC_DEV + row // ROWS_DEV
-    return (section * 256 + (lax.rem(block, 3) - 1) * (ROWS_DEV * 16) + lax.rem(row, ROWS_DEV) * 16)
-
-
-def target_key(tile_row):
-    return float(tile_row // ROWS_DEV * 256 + tile_row % ROWS_DEV * 16)
+def row_key(block, row):
+    section, band = block // 3 - 1, block % 3 - 1
+    return (section * SEC_DEV + row // ROWS_DEV) * 256 + (band * ROWS_DEV + row % ROWS_DEV) * 16
+
+
+def dynamic_key(block, row):
+    section, band = block // 3 - 1, lax.rem(block, 3) - 1
+    key = (section * SEC_DEV + row // ROWS_DEV) * 256 + (band * ROWS_DEV + row % ROWS_DEV) * 16
+    return key.astype(F32)
+
+
+def reach(block, row, target_block, target_row):
+    section = (target_block // 3 - block // 3) * SEC_DEV + target_row // 2 - row // 2
+    across = (target_block % 3 - block % 3) * ROWS_DEV + target_row % 2 - row % 2
+    return abs(section) <= 2 and abs(across) <= 2
+
+
+def turn(value, shift):
+    return pltpu.roll(value, shift % NCOLS, 1) if shift else value
+
+
+def own_keys(terms, moments, keys, moved):
+    for row in range(TILE_ROWS):
+        code = jnp.broadcast_to(moments[4, 0, row, 6:7, :], (8, NCOLS)) + float(row_key(4, row))
+        for i, shift in enumerate(SHIFTS):
+            keys[16 + row, i] = turn(code, shift) - float(shift)
+            moved[row, i] = turn(terms[row], shift)
+
+
+def scatter_to(block, keys, moved, out):
+    for target in range(TILE_ROWS):
+        total = jnp.zeros((8, NCOLS), F32)
+        here = float(row_key(block, target))
+        for row in range(TILE_ROWS):
+            if reach(4, row, block, target):
+                for i in range(5):
+                    total = total + jnp.where(keys[16 + row, i] == here, moved[row, i], 0.0)
+        out(target, total)
+
+
+def gather_blocks(moments, keys):
+    def step(block, totals):
+        totals = list(totals)
+        for row in range(TILE_ROWS):
+            value = moments[block, 1, row]
+            code = jnp.broadcast_to(moments[block, 0, row, 6:7, :], (8, NCOLS))
+            code = code + dynamic_key(block, row)
+            for i, shift in enumerate(SHIFTS):
+                key = turn(code, shift) - float(shift)
+                keys[block * TILE_ROWS + row, i] = key
+                part = turn(value, shift)
+                for t in range(TILE_ROWS):
+                    hit = key == float(row_key(4, t))
+                    totals[t] = totals[t] + jnp.where(hit, part, 0.0)
+        return tuple(totals)
+
+    return lax.fori_loop(0, 9, step, (jnp.zeros((8, NCOLS), F32),) * TILE_ROWS)
+
+
+def own_blocks(block, g):
+    upper, lower = halves(block)
+    line = lax.rem(lax.broadcasted_iota(jnp.int32, (8, NCOLS), 0), 3)
+    xx, xy, yy = (row_of(lower, k, k) for k in range(3))
+    x, y = (row_of(upper, k, k) for k in range(2))
+    first = jnp.where(line == 0, xx, jnp.where(line == 1, xy, jnp.where(line == 2, x, 0.0)))
+    second = jnp.where(line == 0, xy, jnp.where(line == 1, yy, jnp.where(line == 2, y, 0.0)))
+    return first * row_of(g, 0, 3) + second * row_of(g, 1, 4) + upper * row_of(g, 2, 5)
+
+
+def apply_pairs(field, moments, local, keys):
+    def step(block, carry):
+        far, totals = list(carry[:20]), list(carry[20:])
+        for row in range(TILE_ROWS):
+            g = field[block, row]
+            here = dynamic_key(block, row)
+            for t in range(TILE_ROWS):
+                for i in range(5):
+                    far[t * 5 + i] = jnp.where(keys[16 + t, i] == here, g, far[t * 5 + i])
+            by_a, by_b = halves(moments[block, 0, row])
+            by_c, _ = halves(moments[block, 1, row])
+            value = by_a * row_of(g, 0, 3) + by_b * row_of(g, 1, 4) + by_c * row_of(g, 2, 5)
+            for i, shift in enumerate(SHIFTS):
+                part = turn(value, shift)
+                key = keys[block * TILE_ROWS + row, i]
+                for t in range(TILE_ROWS):
+                    hit = key == float(row_key(4, t))
+                    totals[t] = totals[t] + jnp.where(hit, part, 0.0)
+        return tuple(far) + tuple(totals)
+
+    carry = lax.fori_loop(0, 9, step, (jnp.zeros((8, NCOLS), F32),) * 24)
+    out = []
+    for t in range(TILE_ROWS):
+        far = carry[t * 5 + 2]
+        for i, shift in enumerate(SHIFTS):
+            if shift:
+                far = far + turn(carry[t * 5 + i], -shift)
+        by_a, by_b = halves(local[2, t])
+        by_c, _ = halves(local[1, t])
+        near = by_a * row_of(far, 0, 3) + by_b * row_of(far, 1, 4) + by_c * row_of(far, 2, 5)
+        out.append(near + carry[20 + t])
+    return out
 
 
 def kernel(
@@ -163,14 +263,23 @@
     count_ref,
     solution_ref,
     direction_ref,
+    coords,
+    targets,
+    first,
+    second,
+    count,
     table,
     terms,
+    folded,
+    arrived,
     moments,
     local,
     keys,
+    moved,
     field,
     sums_one,
     sums_two,
+    load_sems,
     terms_send,
     terms_recv,
     moments_send,
@@ -206,125 +315,102 @@
     lax.fori_loop(1, group_one, functools.partial(greet, peer_one), 0)
     lax.fori_loop(1, group_two, functools.partial(greet, peer_two), 0)
 
-    squares = pair_tables(coords_ref, targets_ref, first_ref, second_ref, count_ref, table)
+    loads = []
+
+    def load(source, target):
+        loads.append(pltpu.make_async_copy(source, target, load_sems.at[len(loads)]))
+        loads[-1].start()
+
+    load(count_ref, count)
+    load(first_ref, first)
+    load(second_ref, second)
+    blocks = coords_ref.shape[2] // NCOLS
+    for i in range(blocks):
+        lanes = pl.ds(i * NCOLS, NCOLS)
+        load(coords_ref.at[:, :, lanes], coords.at[:, :, lanes])
+        load(targets_ref.at[:, :, lanes], targets.at[:, :, lanes])
+    for copy in loads[:3]:
+        copy.wait()
+
+    def ready(i):
+        loads[3 + 2 * i].wait()
+        loads[4 + 2 * i].wait()
+
+    squares = pair_tables(coords, targets, first, second, count, table, ready)
 
     def store(group, tile_row, value):
         if group == 0:
-            terms[4, tile_row] = value
+            terms[tile_row] = value
         elif group < 3:
             moments[4, group - 1, tile_row] = value
         else:
             local[group - 3, tile_row] = value
 
-    by_first_tile(first_ref, table, store)
+    by_first_tile(first, table, store)
+    own_keys(terms, moments, keys, moved)
 
     pl.semaphore_wait(barrier, 8 + group_one - 1 + group_two - 1)
 
-    def exchange(buffer, send, recv):
-        copies = []
-        for i, (a, b) in enumerate(NEIGHBOURS):
-            copies.append(
-                pltpu.make_async_remote_copy(
-                    src_ref=buffer.at[4],
-                    dst_ref=buffer.at[(1 - a) * 3 + 1 - b],
-                    send_sem=send.at[i],
-                    recv_sem=recv.at[i],
-                    device_id=neighbour(a, b),
-                    device_id_type=MESH,
-                )
-            )
-            copies[-1].start()
-        return copies
-
-    terms_copies = exchange(terms, terms_send, terms_recv)
-    moments_copies = exchange(moments, moments_send, moments_recv)
-    for copy in terms_copies:
-        copy.wait_recv()
-
-    zero = jnp.zeros((8, NCOLS), F32)
-
-    def add_terms(source, totals):
-        totals = list(totals)
-        block, row = source // TILE_ROWS, lax.rem(source, TILE_ROWS)
-        value = terms[block, row]
-        place = jnp.broadcast_to(value[3:4], (8, NCOLS)) + origin(source).astype(F32)
-        for i, shift in enumerate(SHIFTS):
-            moved = pltpu.roll(value, shift % NCOLS, 1)
-            key = pltpu.roll(place, shift % NCOLS, 1) - float(shift)
-            keys[source, i] = key
-            for t in range(TILE_ROWS):
-                totals[t] = totals[t] + jnp.where(key == target_key(t), moved, 0.0)
-        return tuple(totals)
-
-    totals = lax.fori_loop(0, 9 * TILE_ROWS, add_terms, (zero,) * TILE_ROWS)
-    held = lax.rem(lax.broadcasted_iota(jnp.int32, (8, NCOLS), 0), 4) < 3
-    gradient = []
+    def send(source, target, send_sem, recv_sem, i, part=lambda ref: ref.at[:, 0:6]):
+        a, b = NEIGHBOURS[i]
+        copy = pltpu.make_async_remote_copy(
+            src_ref=source,
+            dst_ref=part(target.at[(1 - a) * 3 + 1 - b]),
+            send_sem=send_sem.at[i],
+            recv_sem=recv_sem.at[i],
+            device_id=neighbour(a, b),
+            device_id_type=MESH,
+        )
+        copy.start()
+        return copy
+
+    terms_copies = []
+    for i, (a, b) in enumerate(NEIGHBOURS):
+        block = (a + 1) * 3 + b + 1
+
+        def put(t, value, block=block):
+            folded[block, t] = value
+
+        scatter_to(block, keys, moved, put)
+        terms_copies.append(send(folded.at[block, :, 0:6], arrived, terms_send, terms_recv, i))
+    moments_copies = []
+    for i in range(8):
+        moments_copies.append(send(moments.at[4], moments, moments_send, moments_recv, i, lambda ref: ref))
+
+    gradient = [None] * TILE_ROWS
+
+    def keep(t, value):
+        gradient[t] = value + local[0, t]
+
+    scatter_to(4, keys, moved, keep)
+    for i, (a, b) in enumerate(NEIGHBOURS):
+        terms_copies[i].wait_recv()
+        for t in range(TILE_ROWS):
+            gradient[t] = gradient[t] + arrived[(1 - a) * 3 + 1 - b, t]
+    held = lax.broadcasted_iota(jnp.int32, (8, NCOLS), 0) < 6
     for t in range(TILE_ROWS):
-        gradient.append(jnp.where(held, totals[t] + local[0, t], 0.0))
+        gradient[t] = jnp.where(held, gradient[t], 0.0)
         field[4, t] = gradient[t]
-    field_copies = exchange(field, field_send, field_recv)
+    field_copies = []
+    for i in range(8):
+        field_copies.append(send(field.at[4, :, 0:6], field, field_send, field_recv, i))
 
     for copy in moments_copies:
         copy.wait_recv()
-
-    def add_blocks(source, totals):
-        totals = list(totals)
-        block, row = source // TILE_ROWS, lax.rem(source, TILE_ROWS)
-        value = moments[block, 1, row]
-        for i, shift in enumerate(SHIFTS):
-            moved = pltpu.roll(value, shift % NCOLS, 1)
-            key = keys[source, i]
-            for t in range(TILE_ROWS):
-                totals[t] = totals[t] + jnp.where(key == target_key(t), moved, 0.0)
-        return tuple(totals)
-
-    blocks = lax.fori_loop(0, 9 * TILE_ROWS, add_blocks, (zero,) * TILE_ROWS)
+    zero = jnp.zeros((8, NCOLS), F32)
     gg = zero
     own = []
-    for t in range(TILE_ROWS):
-        g = gradient[t]
-        gg = gg + g * g
-        upper, lower = halves(blocks[t] + local[1, t])
-        line = lax.rem(lax.broadcasted_iota(jnp.int32, (8, NCOLS), 0), 4)
-        xx, xy, yy = (row_of(lower, k, k) for k in range(3))
-        x, y = (row_of(upper, k, k) for k in range(2))
-        first = jnp.where(line == 0, xx, jnp.where(line == 1, xy, jnp.where(line == 2, x, 0.0)))
-        second = jnp.where(line == 0, xy, jnp.where(line == 1, yy, jnp.where(line == 2, y, 0.0)))
-        own.append(first * row_of(g, 0, 4) + second * row_of(g, 1, 5) + upper * row_of(g, 2, 6))
+    for t, block in enumerate(gather_blocks(moments, keys)):
+        gg = gg + gradient[t] * gradient[t]
+        own.append(own_blocks(block + local[1, t], gradient[t]))
 
     for copy in field_copies:
         copy.wait_recv()
-
-    def apply(source, carry):
-        far, totals = list(carry[:20]), list(carry[20:])
-        block, row = source // TILE_ROWS, lax.rem(source, TILE_ROWS)
-        g = field[block, row]
-        here = origin(source).astype(F32)
-        for t in range(TILE_ROWS):
-            for i in range(5):
-                far[t * 5 + i] = jnp.where(keys[16 + t, i] == here, g, far[t * 5 + i])
-        by_a, by_b = halves(moments[block, 0, row])
-        by_c, _ = halves(moments[block, 1, row])
-        value = by_a * row_of(g, 0, 4) + by_b * row_of(g, 1, 5) + by_c * row_of(g, 2, 6)
-        for i, shift in enumerate(SHIFTS):
-            moved = pltpu.roll(value, shift % NCOLS, 1)
-            key = keys[source, i]
-            for t in range(TILE_ROWS):
-                totals[t] = totals[t] + jnp.where(key == target_key(t), moved, 0.0)
-        return tuple(far) + tuple(totals)
-
-    carry = lax.fori_loop(0, 9 * TILE_ROWS, apply, (zero,) * 24)
+    others = apply_pairs(field, moments, local, keys)
     wg, ww = zero, zero
     product = []
     for t in range(TILE_ROWS):
-        far = carry[t * 5 + 2]
-        for i, shift in enumerate(SHIFTS):
-            if shift:
-                far = far + pltpu.roll(carry[t * 5 + i], -shift % NCOLS, 1)
-        by_a, by_b = halves(local[2, t])
-        by_c, _ = halves(local[1, t])
-        near = by_a * row_of(far, 0, 4) + by_b * row_of(far, 1, 5) + by_c * row_of(far, 2, 6)
-        w = jnp.where(held, own[t] - near - carry[20 + t], 0.0)
+        w = jnp.where(held, own[t] - others[t], 0.0)
         product.append(w)
         wg = wg + w * gradient[t]
         ww = ww + w * w
@@ -338,7 +424,9 @@
     def spread_sum(line, buffer, count, peer, i):
         buffer[0:1, :] = line
 
-        def send(d, carry):
+        def send_to(k, carry):
+            step = k // 2
+            d = count // 2 + (2 * lax.rem(k, 2) - 1) * step
             pltpu.make_async_remote_copy(
                 src_ref=buffer.at[pl.ds(0, 1), :],
                 dst_ref=buffer.at[pl.ds(d, 1), :],
@@ -349,7 +437,7 @@
             ).start()
             return carry
 
-        lax.fori_loop(1, count, send, 0)
+        lax.fori_loop(1, count, send_to, 0)
         others = buffer.at[pl.ds(1, count - 1), :]
         pltpu.make_async_copy(others, others, sums_recv.at[i]).wait()
         return jnp.sum(buffer[0:count, :], axis=0, keepdims=True)
@@ -378,7 +466,7 @@
     for t in range(TILE_ROWS):
         one = first_scale * gradient[t]
         two = scale_w * product[t] + scale_g * gradient[t]
-        for k, row in enumerate((0, 1, 2, 4, 5, 6)):
+        for k, row in enumerate(range(6)):
             solution_ref[k, t : t + 1, :] = one[row : row + 1]
             direction_ref[k, t : t + 1, :] = two[row : row + 1]
 
@@ -398,28 +486,38 @@
     def on_device(targets, coords, pair_first, pair_second, pair_count):
         slots, pairs = coords.shape[1], coords.shape[-1]
         vmem = pl.BlockSpec(memory_space=pltpu.VMEM)
+        anywhere = pl.BlockSpec(memory_space=pl.ANY)
         shape = (6, TILE_ROWS, NCOLS)
         tile = (8, NCOLS)
         dma = pltpu.SemaphoreType.DMA
         outputs = pl.pallas_call(
             functools.partial(kernel, sections, bands, group_one),
             out_shape=(jax.ShapeDtypeStruct(shape, F32), jax.ShapeDtypeStruct(shape, F32)),
-            in_specs=[vmem] * 5,
+            in_specs=[anywhere] * 5,
             out_specs=(vmem, vmem),
             scratch_shapes=[
+                pltpu.VMEM((4, slots, pairs), coords.dtype),
+                pltpu.VMEM((2, slots, pairs), targets.dtype),
+                pltpu.VMEM((1, pairs), jnp.int32),
+                pltpu.VMEM((1, pairs), jnp.int32),
+                pltpu.VMEM((1, pairs), jnp.int32),
                 pltpu.VMEM((8 * len(GROUPS), pairs), F32),
+                pltpu.VMEM((TILE_ROWS,) + tile, F32),
+                pltpu.VMEM((9, TILE_ROWS) + tile, F32),
                 pltpu.VMEM((9, TILE_ROWS) + tile, F32),
                 pltpu.VMEM((9, 2, TILE_ROWS) + tile, F32),
                 pltpu.VMEM((3, TILE_ROWS) + tile, F32),
                 pltpu.VMEM((9 * TILE_ROWS, 5) + tile, F32),
+                pltpu.VMEM((TILE_ROWS, 5) + tile, F32),
                 pltpu.VMEM((9, TILE_ROWS) + tile, F32),
                 pltpu.VMEM((group_one, NCOLS), F32),
                 pltpu.VMEM((group_two, NCOLS), F32),
             ]
+            + [dma((3 + 2 * (pairs // NCOLS),))]
             + [dma((8,))] * 6
             + [dma((2,))] * 2,
             compiler_params=pltpu.CompilerParams(
-                collective_id=0, has_side_effects=True, vmem_limit_bytes=32 * 2**20
+                collective_id=0, has_side_effects=True, vmem_limit_bytes=60 * 2**20
             ),
         )(
             coords.reshape(4, slots, pairs),

time: 51.3 us -> 44 us (0.86)
  Pallas kernels: 46.4 us -> 41.2 us
  local copies, waits for them, and re-layouts: 3.95 us -> 1.92 us
    pallas_call x1, Pallas kernels: 46.4 us -> 41.2 us  [on_device(): pl.pallas_call(functools.partial(kernel, sections, bands, group_one), out...]
    unnamed x12 -> x4, local copies, waits for them, and re-layouts: 3.95 us -> 1.92 us
where the time goes in v2:
time: 44 us; the launch traced here: 43.8 us
  Pallas kernels  41.2 us (94%)
  local copies, waits for them, and re-layouts  1.92 us (4%)
  between operations  0.65 us (1%)
    pallas_call x1, Pallas kernels, on_device(): pl.pallas_call(functools.partial(kernel, sections, bands, group_one), out...  41.2 us
    unnamed x4, local copies, waits for them, and re-layouts  1.92 us

profile of v2, /device:TPU:1, one launch (start us, length us, event | category | flops | bytes accessed | tf_op | source)
XLA Modules:
  0.0 43.8 jit_solution(5771356429557067977)
XLA Ops:
  0.6 41.2 %shard_map.68 = (f32[6,4,128]{2,1,0:T(4,128)}, f32[6,4,128]{2,1,0:T(4,128)}) custom-call(bf16[4,160,512]{2,1,0:T(8,128)(2,1)} %bitcast.7, bf16[2,160,512]{2,1,0:T(8,128)(2,1)} %bitcast.8, s32[1,512]{1,0:T(1,128)} %bitcast.11, s32[1,512]{1,0:T(1,128)} %bitcast.12, s32[1,512]{1,0:T(1,128)} %bitcast.13), custom_call_target="tpu_custom_call" | custom-call | tf_op jit(solution)/shard_map/pallas_call | solution.py:493
  41.8 0.0 copy-start
  41.8 1.3 %copy.9 = f32[6,2,2,128]{3,2,1,0:T(2,128)} copy(f32[6,2,2,128]{3,2,1,0:T(2,128)} %bitcast.10) | data formatting | bytes 24576
  43.1 0.0 copy-done
  43.2 0.6 %copy.10 = f32[6,2,2,128]{3,2,1,0:T(2,128)} copy(f32[6,2,2,128]{3,2,1,0:T(2,128)S(1)} %bitcast.9) | data formatting | bytes 24576
Async XLA Ops:
  41.8 1.3 %copy-start = (f32[6,4,128]{2,1,0:T(4,128)S(1)}, f32[6,4,128]{2,1,0:T(4,128)}, u32[]{:S(2)}) copy-start(f32[6,4,128]{2,1,0:T(4,128)} %get-tuple-element.5) | copy-start | bytes 36868

commit v3 on v2

--- a/solution.py
+++ b/solution.py
@@ -15,9 +15,12 @@
 ROWS_WIDE = ROWS_DEV + 4
 MESH = pl.DeviceIdType.MESH
 CHUNKS = 5
+VMEM_BYTES = 56426496
 F32 = jnp.float32
 SHIFTS = (-2, -1, 0, 1, 2)
-NEIGHBOURS = ((-1, -1), (1, -1), (-1, 1), (1, 1), (-1, 0), (1, 0), (0, -1), (0, 1))
+EDGES = (1, 3, 5, 7)
+CORNERS = (0, 2, 6, 8)
+NEIGHBOURS = ((-1, 0), (1, 0), (0, -1), (0, 1), (-1, -1), (1, -1), (-1, 1), (1, 1))
 
 SUMS = (
     "xp",
@@ -128,25 +131,30 @@
     return squares
 
 
-def by_first_tile(first_ref, table, store):
+def place_table(first_ref, chosen):
+    pairs = first_ref.shape[1]
+    first = jnp.broadcast_to(first_ref[...], (NCOLS, pairs))
+    column = lax.broadcasted_iota(jnp.int32, (NCOLS, pairs), 0)
+    for row in range(TILE_ROWS):
+        start = ((row // ROWS_DEV + 2) * ROWS_WIDE + row % ROWS_DEV + 2) * NCOLS
+        chosen[row] = jnp.where(first == column + start, 1.0, 0.0).astype(jnp.bfloat16)
+
+
+def by_first_tile(chosen, table, store):
     values = table[...]
     high = values.astype(jnp.bfloat16)
     rest = values - high.astype(F32)
     middle = rest.astype(jnp.bfloat16)
     low = (rest - middle.astype(F32)).astype(jnp.bfloat16)
     parts = jnp.concatenate([high, middle, low], axis=0)
-    height, pairs = values.shape
-    first = jnp.broadcast_to(first_ref[...], (NCOLS, pairs))
-    column = lax.broadcasted_iota(jnp.int32, (NCOLS, pairs), 0)
-    for tile_row in range(TILE_ROWS):
-        start = ((tile_row // ROWS_DEV + 2) * ROWS_WIDE + tile_row % ROWS_DEV + 2) * NCOLS
-        chosen = jnp.where(first == column + start, 1.0, 0.0).astype(jnp.bfloat16)
+    height = values.shape[0]
+    for row in range(TILE_ROWS):
         moved = lax.dot_general(
-            parts, chosen, (((1,), (1,)), ((), ())), preferred_element_type=F32
+            parts, chosen[row], (((1,), (1,)), ((), ())), preferred_element_type=F32
         )
         moved = moved[:height] + moved[height : 2 * height] + moved[2 * height :]
         for group in range(len(GROUPS)):
-            store(group, tile_row, moved[8 * group : 8 * group + 8])
+            store(group, row, moved[8 * group : 8 * group + 8])
 
 
 def row_key(block, row):
@@ -218,7 +226,7 @@
     return first * row_of(g, 0, 3) + second * row_of(g, 1, 4) + upper * row_of(g, 2, 5)
 
 
-def apply_pairs(field, moments, local, keys):
+def apply_pairs(field, moments, local, keys, landed):
     def step(block, carry):
         far, totals = list(carry[:20]), list(carry[20:])
         for row in range(TILE_ROWS):
@@ -238,7 +246,18 @@
                     totals[t] = totals[t] + jnp.where(hit, part, 0.0)
         return tuple(far) + tuple(totals)
 
-    carry = lax.fori_loop(0, 9, step, (jnp.zeros((8, NCOLS), F32),) * 24)
+    def edge(k, carry):
+        landed(2 * k + 1)
+        return step(2 * k + 1, carry)
+
+    def corner(k, carry):
+        block = 2 * k + 2 * (k // 2)
+        landed(block)
+        return step(block, carry)
+
+    carry = step(jnp.int32(4), (jnp.zeros((8, NCOLS), F32),) * 24)
+    carry = lax.fori_loop(0, len(EDGES), edge, carry)
+    carry = lax.fori_loop(0, len(CORNERS), corner, carry)
     out = []
     for t in range(TILE_ROWS):
         far = carry[t * 5 + 2]
@@ -261,13 +280,17 @@
     first_ref,
     second_ref,
     count_ref,
-    solution_ref,
-    direction_ref,
+    gradient_ref,
+    product_ref,
+    solution_scale_ref,
+    product_scale_ref,
+    gradient_scale_ref,
     coords,
     targets,
     first,
     second,
     count,
+    chosen,
     table,
     terms,
     folded,
@@ -331,6 +354,7 @@
         load(targets_ref.at[:, :, lanes], targets.at[:, :, lanes])
     for copy in loads[:3]:
         copy.wait()
+    place_table(first, chosen)
 
     def ready(i):
         loads[3 + 2 * i].wait()
@@ -346,7 +370,7 @@
         else:
             local[group - 3, tile_row] = value
 
-    by_first_tile(first, table, store)
+    by_first_tile(chosen, table, store)
     own_keys(terms, moments, keys, moved)
 
     pl.semaphore_wait(barrier, 8 + group_one - 1 + group_two - 1)
@@ -357,13 +381,16 @@
             src_ref=source,
             dst_ref=part(target.at[(1 - a) * 3 + 1 - b]),
             send_sem=send_sem.at[i],
-            recv_sem=recv_sem.at[i],
+            recv_sem=recv_sem.at[(1 - a) * 3 + 1 - b],
             device_id=neighbour(a, b),
             device_id_type=MESH,
         )
         copy.start()
         return copy
 
+    def landed(ref, sem):
+        pltpu.make_async_copy(ref, ref, sem).wait()
+
     terms_copies = []
     for i, (a, b) in enumerate(NEIGHBOURS):
         block = (a + 1) * 3 + b + 1
@@ -383,10 +410,10 @@
         gradient[t] = value + local[0, t]
 
     scatter_to(4, keys, moved, keep)
-    for i, (a, b) in enumerate(NEIGHBOURS):
-        terms_copies[i].wait_recv()
+    for block in EDGES + CORNERS:
+        landed(arrived.at[block, :, 0:6], terms_recv.at[block])
         for t in range(TILE_ROWS):
-            gradient[t] = gradient[t] + arrived[(1 - a) * 3 + 1 - b, t]
+            gradient[t] = gradient[t] + arrived[block, t]
     held = lax.broadcasted_iota(jnp.int32, (8, NCOLS), 0) < 6
     for t in range(TILE_ROWS):
         gradient[t] = jnp.where(held, gradient[t], 0.0)
@@ -395,8 +422,8 @@
     for i in range(8):
         field_copies.append(send(field.at[4, :, 0:6], field, field_send, field_recv, i))
 
-    for copy in moments_copies:
-        copy.wait_recv()
+    for block in EDGES + CORNERS:
+        landed(moments.at[block], moments_recv.at[block])
     zero = jnp.zeros((8, NCOLS), F32)
     gg = zero
     own = []
@@ -404,9 +431,10 @@
         gg = gg + gradient[t] * gradient[t]
         own.append(own_blocks(block + local[1, t], gradient[t]))
 
-    for copy in field_copies:
-        copy.wait_recv()
-    others = apply_pairs(field, moments, local, keys)
+    def field_landed(block):
+        landed(field.at[block, :, 0:6], field_recv.at[block])
+
+    others = apply_pairs(field, moments, local, keys, field_landed)
     wg, ww = zero, zero
     product = []
     for t in range(TILE_ROWS):
@@ -414,6 +442,11 @@
         product.append(w)
         wg = wg + w * gradient[t]
         ww = ww + w * w
+
+    for t in range(TILE_ROWS):
+        for k in range(6):
+            gradient_ref[k, t : t + 1, :] = gradient[t][k : k + 1]
+            product_ref[k, t : t + 1, :] = product[t][k : k + 1]
 
     lane = lax.broadcasted_iota(jnp.int32, (1, NCOLS), 1)
     line = jnp.zeros((1, NCOLS), F32)
@@ -445,10 +478,7 @@
     line = spread_sum(line, sums_one, group_one, peer_one, 0)
     line = spread_sum(line, sums_two, group_two, peer_two, 1)
 
-    def total_of(k):
-        return jnp.sum(jnp.where(lane == k, line, 0.0), axis=1, keepdims=True)
-
-    rr, gg, wg, ww = (total_of(k) for k in range(4))
+    rr, gg, wg, ww = (jnp.broadcast_to(line[:, k : k + 1], (1, NCOLS)) for k in range(4))
     beta_one = jnp.sqrt(rr)
     norm_g = jnp.sqrt(gg)
     alpha_one = norm_g / beta_one
@@ -463,12 +493,9 @@
     root = math.sqrt(float(6 * TILE_ROWS * NCOLS * sections * bands))
     scale_w = root * on_w / alpha_two
     scale_g = root * (on_g / alpha_two - beta_two * alpha_two / (rho_sq * norm_g))
-    for t in range(TILE_ROWS):
-        one = first_scale * gradient[t]
-        two = scale_w * product[t] + scale_g * gradient[t]
-        for k, row in enumerate(range(6)):
-            solution_ref[k, t : t + 1, :] = one[row : row + 1]
-            direction_ref[k, t : t + 1, :] = two[row : row + 1]
+    solution_scale_ref[...] = first_scale
+    product_scale_ref[...] = scale_w
+    gradient_scale_ref[...] = scale_g
 
     for copies in (terms_copies, moments_copies, field_copies):
         for copy in copies:
@@ -490,17 +517,18 @@
         shape = (6, TILE_ROWS, NCOLS)
         tile = (8, NCOLS)
         dma = pltpu.SemaphoreType.DMA
-        outputs = pl.pallas_call(
+        gradient, product, *scales = pl.pallas_call(
             functools.partial(kernel, sections, bands, group_one),
-            out_shape=(jax.ShapeDtypeStruct(shape, F32), jax.ShapeDtypeStruct(shape, F32)),
+            out_shape=tuple(jax.ShapeDtypeStruct(s, F32) for s in (shape, shape) + ((1, NCOLS),) * 3),
             in_specs=[anywhere] * 5,
-            out_specs=(vmem, vmem),
+            out_specs=(vmem,) * 5,
             scratch_shapes=[
                 pltpu.VMEM((4, slots, pairs), coords.dtype),
                 pltpu.VMEM((2, slots, pairs), targets.dtype),
                 pltpu.VMEM((1, pairs), jnp.int32),
                 pltpu.VMEM((1, pairs), jnp.int32),
                 pltpu.VMEM((1, pairs), jnp.int32),
+                pltpu.VMEM((TILE_ROWS, NCOLS, pairs), jnp.bfloat16),
                 pltpu.VMEM((8 * len(GROUPS), pairs), F32),
                 pltpu.VMEM((TILE_ROWS,) + tile, F32),
                 pltpu.VMEM((9, TILE_ROWS) + tile, F32),
@@ -514,10 +542,10 @@
                 pltpu.VMEM((group_two, NCOLS), F32),
             ]
             + [dma((3 + 2 * (pairs // NCOLS),))]
-            + [dma((8,))] * 6
+            + [dma((8,)), dma((9,))] * 3
             + [dma((2,))] * 2,
             compiler_params=pltpu.CompilerParams(
-                collective_id=0, has_side_effects=True, vmem_limit_bytes=60 * 2**20
+                collective_id=0, has_side_effects=True, vmem_limit_bytes=VMEM_BYTES
             ),
         )(
             coords.reshape(4, slots, pairs),
@@ -526,7 +554,9 @@
             pair_second.reshape(1, pairs),
             pair_count.reshape(1, pairs),
         )
-        return tuple(o.reshape(6, SEC_DEV, ROWS_DEV, NCOLS) for o in outputs)
+        first_scale, scale_w, scale_g = (scale[None] for scale in scales)
+        results = (first_scale * gradient, scale_w * product + scale_g * gradient)
+        return tuple(x.reshape(6, SEC_DEV, ROWS_DEV, NCOLS) for x in results)
 
     return jax.shard_map(
         on_device,

time: 44 us -> 42.3 us (0.961)
  local copies, waits for them, and re-layouts: 1.92 us -> 0.69 us
  Pallas kernels: 41.2 us -> 40.2 us
  other arithmetic: 0 us -> 0.61 us
    unnamed x4 -> x6, local copies, waits for them, and re-layouts: 1.92 us -> 0.69 us
    pallas_call x1, Pallas kernels: 41.2 us -> 40.2 us  [on_device(): pl.pallas_call(functools.partial(kernel, sections, bands, group_one), out...]
    add x0 -> x1, other arithmetic: none -> 0.61 us  [on_device(): results = (first_scale * gradient, scale_w * product + scale_g * gradient)]
where the time goes in v3:
time: 42.3 us; the launch traced here: 42.1 us
  Pallas kernels  40.2 us (95%)
  local copies, waits for them, and re-layouts  0.69 us (2%)
  between operations  0.66 us (2%)
  other arithmetic  0.61 us (1%)
    pallas_call x1, Pallas kernels, on_device(): pl.pallas_call(functools.partial(kernel, sections, bands, group_one), out...  40.2 us

profile of v3, /device:TPU:1, one launch (start us, length us, event | category | flops | bytes accessed | tf_op | source)
XLA Modules:
  0.0 42.1 jit_solution(5487172018626790731)
XLA Ops:
  0.6 0.0 copy-start.2
  0.6 0.0 copy-start.1
  0.7 0.0 copy-start
  0.7 0.7 %copy-done.2 = s32[1,1,512]{2,1,0:T(1,128)S(1)} copy-done((s32[1,1,512]{2,1,0:T(1,128)S(1)}, s32[1,1,512]{2,1,0:T(1,128)}, u32[]{:S(2)}) %copy-start.2) | copy-done | bytes 2072
  1.3 0.0 copy-done.1
  1.3 0.0 copy-done
  1.3 40.2 %shard_map.68 = (f32[6,4,128]{2,1,0:T(4,128)S(1)}, f32[6,4,128]{2,1,0:T(4,128)S(1)}, f32[1,128]{1,0:T(1,128)S(1)}, f32[1,128]{1,0:T(1,128)S(1)}, f32[1,128]{1,0:T(1,128)S(1)}) custom-call(bf16[4,160,512]{2,1,0:T(8,128)(2,1)} %bitcast.16, bf16[2,160,512]{2,1,0:T(8,128)(2,1)} %bitcast.17, s32[1,512]{1,0:T(1,128)S(1)} %bitcast.10, s32[1,512]{1,0:T(1,128)S(1)} %bitcast.11, ...), custom_call_target="tpu_custom_call" | custom-call | tf_op jit(solution)/shard_map/pallas_call | solution.py:520
  41.5 0.6 %multiply_add_fusion = (f32[6,4,128]{2,1,0:T(4,128)}, f32[6,4,128]{2,1,0:T(4,128)}) fusion(f32[6,4,128]{2,1,0:T(4,128)S(1)} %get-tuple-element.8, f32[6,4,128]{2,1,0:T(4,128)S(1)} %get-tuple-element.10, f32[128]{0:T(128)S(1)} %bitcast.15, f32[128]{0:T(128)S(1)} %bitcast.14, f32[128]{0:T(128)S(1)} %bitcast.13), kind=kLoop, calls=%fused_computation | loop fusion | flops 12288 | bytes 50688 | tf_op jit(solution)/shard_map/add | solution.py:558
Async XLA Ops:
  0.6 0.7 %copy-start.2 = (s32[1,1,512]{2,1,0:T(1,128)S(1)}, s32[1,1,512]{2,1,0:T(1,128)}, u32[]{:S(2)}) copy-start(s32[1,1,512]{2,1,0:T(1,128)} %param.9) | copy-start | bytes 6148
  0.6 0.7 %copy-start.1 = (s32[1,1,512]{2,1,0:T(1,128)S(1)}, s32[1,1,512]{2,1,0:T(1,128)}, u32[]{:S(2)}) copy-start(s32[1,1,512]{2,1,0:T(1,128)} %param.8) | copy-start | bytes 6148
  0.7 0.7 %copy-start = (s32[1,1,512]{2,1,0:T(1,128)S(1)}, s32[1,1,512]{2,1,0:T(1,128)}, u32[]{:S(2)}) copy-start(s32[1,1,512]{2,1,0:T(1,128)} %param.7) | copy-start | bytes 6148

commit v4 on v3

--- a/solution.py
+++ b/solution.py
@@ -311,32 +311,62 @@
     field_recv,
     sums_send,
     sums_recv,
+    met,
 ):
     sec = lax.axis_index("sec")
     band = lax.axis_index("band")
-    group_two = sections // group_one * bands
+    place = lax.rem(sec, group_one)
+    base = sec - place
+    group = lax.div(sec, group_one)
 
     def neighbour(a, b):
         return (lax.rem(sec + a + sections, sections), lax.rem(band + b + bands, bands))
 
-    def peer_one(d):
-        base = sec // group_one * group_one
-        return (base + lax.rem(lax.rem(sec, group_one) + d, group_one), band)
-
-    def peer_two(d):
-        i = lax.rem(sec // group_one * bands + band + d, group_two)
-        return (i // bands * group_one + lax.rem(sec, group_one), lax.rem(i, bands))
+    groups = sections // group_one
+
+    def far_first(k, count):
+        return count // 2 + (2 * lax.rem(k, 2) - 1) * lax.div(k + 1, 2)
+
+    def each_peer_one(act):
+        def step(k, carry):
+            act((base + lax.rem(place + far_first(k, group_one), group_one), band))
+            return carry
+
+        lax.fori_loop(0, group_one - 1, step, 0)
+
+    def each_peer_two(act):
+        def step(k, carry):
+            other = lax.rem(group + far_first(k, groups), groups) * group_one + place
+            for x in range(bands):
+                act((other, x))
+            return carry
+
+        lax.fori_loop(0, groups - 1, step, 0)
+        for x in range(1, bands):
+            act((sec, lax.rem(band + x, bands)))
+
+    def half(count):
+        return (count // 2 + 1) // 2
+
+    def each_relay(act):
+        for d in range(1, half(group_one) + 1):
+            for step in (d, group_one - d):
+                act((base + lax.rem(place + step, group_one), band))
+        for d in range(-half(groups), half(groups) + 1):
+            other = lax.rem(group + d + groups, groups) * group_one + place
+            for x in range(-half(bands), half(bands) + 1):
+                if (d, x) != (0, 0):
+                    act((other, lax.rem(band + x + bands, bands)))
+
+    relays = 2 * half(group_one) + (2 * half(groups) + 1) * (2 * half(bands) + 1) - 1
+
+    def signal(semaphore, device):
+        pl.semaphore_signal(semaphore, inc=1, device_id=device, device_id_type=MESH)
 
     barrier = pltpu.get_barrier_semaphore()
+    each_relay(functools.partial(signal, barrier))
     for a, b in NEIGHBOURS:
-        pl.semaphore_signal(barrier, inc=1, device_id=neighbour(a, b), device_id_type=MESH)
-
-    def greet(peer, d, carry):
-        pl.semaphore_signal(barrier, inc=1, device_id=peer(d), device_id_type=MESH)
-        return carry
-
-    lax.fori_loop(1, group_one, functools.partial(greet, peer_one), 0)
-    lax.fori_loop(1, group_two, functools.partial(greet, peer_two), 0)
+        signal(barrier, neighbour(a, b))
 
     loads = []
 
@@ -373,7 +403,7 @@
     by_first_tile(chosen, table, store)
     own_keys(terms, moments, keys, moved)
 
-    pl.semaphore_wait(barrier, 8 + group_one - 1 + group_two - 1)
+    pl.semaphore_wait(barrier, 8 + relays)
 
     def send(source, target, send_sem, recv_sem, i, part=lambda ref: ref.at[:, 0:6]):
         a, b = NEIGHBOURS[i]
@@ -404,6 +434,8 @@
     for i in range(8):
         moments_copies.append(send(moments.at[4], moments, moments_send, moments_recv, i, lambda ref: ref))
 
+    each_relay(functools.partial(signal, met))
+
     gradient = [None] * TILE_ROWS
 
     def keep(t, value):
@@ -454,29 +486,28 @@
         total = jnp.sum(jnp.sum(part, axis=0, keepdims=True), axis=1, keepdims=True)
         line = jnp.where(lane == k, total, line)
 
-    def spread_sum(line, buffer, count, peer, i):
-        buffer[0:1, :] = line
-
-        def send_to(k, carry):
-            step = k // 2
-            d = count // 2 + (2 * lax.rem(k, 2) - 1) * step
+    def spread_sum(line, buffer, each_peer, mine, i):
+        own = buffer.at[pl.ds(mine, 1), :]
+        buffer[pl.ds(mine, 1), :] = line
+
+        def send_to(device):
             pltpu.make_async_remote_copy(
-                src_ref=buffer.at[pl.ds(0, 1), :],
-                dst_ref=buffer.at[pl.ds(d, 1), :],
+                src_ref=own,
+                dst_ref=own,
                 send_sem=sums_send.at[i],
                 recv_sem=sums_recv.at[i],
-                device_id=peer(d),
+                device_id=device,
                 device_id_type=MESH,
             ).start()
-            return carry
-
-        lax.fori_loop(1, count, send_to, 0)
-        others = buffer.at[pl.ds(1, count - 1), :]
+
+        each_peer(send_to)
+        others = buffer.at[pl.ds(1, buffer.shape[0] - 1), :]
         pltpu.make_async_copy(others, others, sums_recv.at[i]).wait()
-        return jnp.sum(buffer[0:count, :], axis=0, keepdims=True)
-
-    line = spread_sum(line, sums_one, group_one, peer_one, 0)
-    line = spread_sum(line, sums_two, group_two, peer_two, 1)
+        return jnp.sum(buffer[...], axis=0, keepdims=True)
+
+    pl.semaphore_wait(met, relays)
+    line = spread_sum(line, sums_one, each_peer_one, place, 0)
+    line = spread_sum(line, sums_two, each_peer_two, group * bands + band, 1)
 
     rr, gg, wg, ww = (jnp.broadcast_to(line[:, k : k + 1], (1, NCOLS)) for k in range(4))
     beta_one = jnp.sqrt(rr)
@@ -500,8 +531,8 @@
     for copies in (terms_copies, moments_copies, field_copies):
         for copy in copies:
             copy.wait_send()
-    for buffer, count, i in ((sums_one, group_one, 0), (sums_two, group_two, 1)):
-        others = buffer.at[pl.ds(1, count - 1), :]
+    for i, buffer in enumerate((sums_one, sums_two)):
+        others = buffer.at[pl.ds(1, buffer.shape[0] - 1), :]
         pltpu.make_async_copy(others, others, sums_send.at[i]).wait()
 
 
@@ -543,7 +574,8 @@
             ]
             + [dma((3 + 2 * (pairs // NCOLS),))]
             + [dma((8,)), dma((9,))] * 3
-            + [dma((2,))] * 2,
+            + [dma((2,))] * 2
+            + [pltpu.SemaphoreType.REGULAR],
             compiler_params=pltpu.CompilerParams(
                 collective_id=0, has_side_effects=True, vmem_limit_bytes=VMEM_BYTES
             ),

time: 42.3 us -> 39.9 us (0.943)
  Pallas kernels: 40.2 us -> 37.8 us
    pallas_call x1, Pallas kernels: 40.2 us -> 37.8 us  [on_device(): pl.pallas_call(functools.partial(kernel, sections, bands, group_one), out...]
where the time goes in v4:
time: 39.9 us; the launch traced here: 39.8 us
  Pallas kernels  37.8 us (95%)
  local copies, waits for them, and re-layouts  0.69 us (2%)
  between operations  0.66 us (2%)
  other arithmetic  0.61 us (2%)
    pallas_call x1, Pallas kernels, on_device(): pl.pallas_call(functools.partial(kernel, sections, bands, group_one), out...  37.8 us

profile of v4, /device:TPU:1, one launch (start us, length us, event | category | flops | bytes accessed | tf_op | source)
XLA Modules:
  0.0 39.8 jit_solution(14241173196147774875)
XLA Ops:
  0.6 0.0 copy-start.2
  0.6 0.0 copy-start.1
  0.7 0.0 copy-start
  0.7 0.7 %copy-done.2 = s32[1,1,512]{2,1,0:T(1,128)S(1)} copy-done((s32[1,1,512]{2,1,0:T(1,128)S(1)}, s32[1,1,512]{2,1,0:T(1,128)}, u32[]{:S(2)}) %copy-start.2) | copy-done | bytes 2072
  1.3 0.0 copy-done.1
  1.3 0.0 copy-done
  1.3 37.8 %shard_map.68 = (f32[6,4,128]{2,1,0:T(4,128)S(1)}, f32[6,4,128]{2,1,0:T(4,128)S(1)}, f32[1,128]{1,0:T(1,128)S(1)}, f32[1,128]{1,0:T(1,128)S(1)}, f32[1,128]{1,0:T(1,128)S(1)}) custom-call(bf16[4,160,512]{2,1,0:T(8,128)(2,1)} %bitcast.16, bf16[2,160,512]{2,1,0:T(8,128)(2,1)} %bitcast.17, s32[1,512]{1,0:T(1,128)S(1)} %bitcast.10, s32[1,512]{1,0:T(1,128)S(1)} %bitcast.11, ...), custom_call_target="tpu_custom_call" | custom-call | tf_op jit(solution)/shard_map/pallas_call | solution.py:551
  39.2 0.6 %multiply_add_fusion = (f32[6,4,128]{2,1,0:T(4,128)}, f32[6,4,128]{2,1,0:T(4,128)}) fusion(f32[6,4,128]{2,1,0:T(4,128)S(1)} %get-tuple-element.8, f32[6,4,128]{2,1,0:T(4,128)S(1)} %get-tuple-element.10, f32[128]{0:T(128)S(1)} %bitcast.15, f32[128]{0:T(128)S(1)} %bitcast.14, f32[128]{0:T(128)S(1)} %bitcast.13), kind=kLoop, calls=%fused_computation | loop fusion | flops 12288 | bytes 50688 | tf_op jit(solution)/shard_map/add | solution.py:590
Async XLA Ops:
  0.6 0.7 %copy-start.2 = (s32[1,1,512]{2,1,0:T(1,128)S(1)}, s32[1,1,512]{2,1,0:T(1,128)}, u32[]{:S(2)}) copy-start(s32[1,1,512]{2,1,0:T(1,128)} %param.9) | copy-start | bytes 6148
  0.6 0.7 %copy-start.1 = (s32[1,1,512]{2,1,0:T(1,128)S(1)}, s32[1,1,512]{2,1,0:T(1,128)}, u32[]{:S(2)}) copy-start(s32[1,1,512]{2,1,0:T(1,128)} %param.8) | copy-start | bytes 6148
  0.7 0.7 %copy-start = (s32[1,1,512]{2,1,0:T(1,128)S(1)}, s32[1,1,512]{2,1,0:T(1,128)}, u32[]{:S(2)}) copy-start(s32[1,1,512]{2,1,0:T(1,128)} %param.7) | copy-start | bytes 6148

commit v5 on v4

--- a/solution.py
+++ b/solution.py
@@ -322,6 +322,20 @@
     def neighbour(a, b):
         return (lax.rem(sec + a + sections, sections), lax.rem(band + b + bands, bands))
 
+    loads = []
+
+    def load(source, target):
+        loads.append(pltpu.make_async_copy(source, target, load_sems.at[len(loads)]))
+        loads[-1].start()
+
+    load(count_ref, count)
+    load(first_ref, first)
+    load(second_ref, second)
+    blocks = coords_ref.shape[2] // NCOLS
+    for i in range(blocks):
+        lanes = pl.ds(i * NCOLS, NCOLS)
+        load(coords_ref.at[:, :, lanes], coords.at[:, :, lanes])
+        load(targets_ref.at[:, :, lanes], targets.at[:, :, lanes])
     groups = sections // group_one
 
     def far_first(k, count):
@@ -368,20 +382,6 @@
     for a, b in NEIGHBOURS:
         signal(barrier, neighbour(a, b))
 
-    loads = []
-
-    def load(source, target):
-        loads.append(pltpu.make_async_copy(source, target, load_sems.at[len(loads)]))
-        loads[-1].start()
-
-    load(count_ref, count)
-    load(first_ref, first)
-    load(second_ref, second)
-    blocks = coords_ref.shape[2] // NCOLS
-    for i in range(blocks):
-        lanes = pl.ds(i * NCOLS, NCOLS)
-        load(coords_ref.at[:, :, lanes], coords.at[:, :, lanes])
-        load(targets_ref.at[:, :, lanes], targets.at[:, :, lanes])
     for copy in loads[:3]:
         copy.wait()
     place_table(first, chosen)
@@ -402,6 +402,16 @@
 
     by_first_tile(chosen, table, store)
     own_keys(terms, moments, keys, moved)
+    gradient = [None] * TILE_ROWS
+    for block in range(9):
+
+        def put(t, value, block=block):
+            if block == 4:
+                gradient[t] = value + local[0, t]
+            else:
+                folded[block, t] = value
+
+        scatter_to(block, keys, moved, put)
 
     pl.semaphore_wait(barrier, 8 + relays)
 
@@ -423,25 +433,14 @@
 
     terms_copies = []
     for i, (a, b) in enumerate(NEIGHBOURS):
-        block = (a + 1) * 3 + b + 1
-
-        def put(t, value, block=block):
-            folded[block, t] = value
-
-        scatter_to(block, keys, moved, put)
-        terms_copies.append(send(folded.at[block, :, 0:6], arrived, terms_send, terms_recv, i))
+        source = folded.at[(a + 1) * 3 + b + 1, :, 0:6]
+        terms_copies.append(send(source, arrived, terms_send, terms_recv, i))
     moments_copies = []
     for i in range(8):
         moments_copies.append(send(moments.at[4], moments, moments_send, moments_recv, i, lambda ref: ref))
 
     each_relay(functools.partial(signal, met))
 
-    gradient = [None] * TILE_ROWS
-
-    def keep(t, value):
-        gradient[t] = value + local[0, t]
-
-    scatter_to(4, keys, moved, keep)
     for block in EDGES + CORNERS:
         landed(arrived.at[block, :, 0:6], terms_recv.at[block])
         for t in range(TILE_ROWS):
@@ -463,6 +462,12 @@
         gg = gg + gradient[t] * gradient[t]
         own.append(own_blocks(block + local[1, t], gradient[t]))
 
+    def whole(part):
+        return jnp.sum(jnp.sum(part, axis=0, keepdims=True), axis=1, keepdims=True)
+
+    lane = lax.broadcasted_iota(jnp.int32, (1, NCOLS), 1)
+    line = jnp.where(lane == 0, whole(squares), jnp.where(lane == 1, whole(gg), 0.0))
+
     def field_landed(block):
         landed(field.at[block, :, 0:6], field_recv.at[block])
 
@@ -475,18 +480,16 @@
         wg = wg + w * gradient[t]
         ww = ww + w * w
 
-    for t in range(TILE_ROWS):
-        for k in range(6):
-            gradient_ref[k, t : t + 1, :] = gradient[t][k : k + 1]
-            product_ref[k, t : t + 1, :] = product[t][k : k + 1]
-
-    lane = lax.broadcasted_iota(jnp.int32, (1, NCOLS), 1)
-    line = jnp.zeros((1, NCOLS), F32)
-    for k, part in enumerate((squares, gg, wg, ww)):
-        total = jnp.sum(jnp.sum(part, axis=0, keepdims=True), axis=1, keepdims=True)
-        line = jnp.where(lane == k, total, line)
-
-    def spread_sum(line, buffer, each_peer, mine, i):
+    for k, part in ((2, wg), (3, ww)):
+        line = jnp.where(lane == k, whole(part), line)
+
+    def store_results():
+        for t in range(TILE_ROWS):
+            for k in range(6):
+                gradient_ref[k, t : t + 1, :] = gradient[t][k : k + 1]
+                product_ref[k, t : t + 1, :] = product[t][k : k + 1]
+
+    def spread_sum(line, buffer, each_peer, mine, i, meanwhile):
         own = buffer.at[pl.ds(mine, 1), :]
         buffer[pl.ds(mine, 1), :] = line
 
@@ -501,13 +504,14 @@
             ).start()
 
         each_peer(send_to)
+        meanwhile()
         others = buffer.at[pl.ds(1, buffer.shape[0] - 1), :]
         pltpu.make_async_copy(others, others, sums_recv.at[i]).wait()
         return jnp.sum(buffer[...], axis=0, keepdims=True)
 
     pl.semaphore_wait(met, relays)
-    line = spread_sum(line, sums_one, each_peer_one, place, 0)
-    line = spread_sum(line, sums_two, each_peer_two, group * bands + band, 1)
+    line = spread_sum(line, sums_one, each_peer_one, place, 0, store_results)
+    line = spread_sum(line, sums_two, each_peer_two, group * bands + band, 1, lambda: None)
 
     rr, gg, wg, ww = (jnp.broadcast_to(line[:, k : k + 1], (1, NCOLS)) for k in range(4))
     beta_one = jnp.sqrt(rr)

time: 39.9 us -> 39.9 us (level)
  no operation moved by 1% of the time
where the time goes in v5:
time: 39.9 us; the launch traced here: 39.7 us
  Pallas kernels  37.8 us (95%)
  local copies, waits for them, and re-layouts  0.69 us (2%)
  between operations  0.66 us (2%)
  other arithmetic  0.61 us (2%)
    pallas_call x1, Pallas kernels, on_device(): pl.pallas_call(functools.partial(kernel, sections, bands, group_one), out...  37.8 us

profile of v5, /device:TPU:1, one launch (start us, length us, event | category | flops | bytes accessed | tf_op | source)
XLA Modules:
  0.0 39.7 jit_solution(1617523447079352653)
XLA Ops:
  0.6 0.0 copy-start.2
  0.6 0.0 copy-start.1
  0.7 0.0 copy-start
  0.7 0.7 %copy-done.2 = s32[1,1,512]{2,1,0:T(1,128)S(1)} copy-done((s32[1,1,512]{2,1,0:T(1,128)S(1)}, s32[1,1,512]{2,1,0:T(1,128)}, u32[]{:S(2)}) %copy-start.2) | copy-done | bytes 2072
  1.3 0.0 copy-done.1
  1.3 0.0 copy-done
  1.3 37.8 %shard_map.68 = (f32[6,4,128]{2,1,0:T(4,128)S(1)}, f32[6,4,128]{2,1,0:T(4,128)S(1)}, f32[1,128]{1,0:T(1,128)S(1)}, f32[1,128]{1,0:T(1,128)S(1)}, f32[1,128]{1,0:T(1,128)S(1)}) custom-call(bf16[4,160,512]{2,1,0:T(8,128)(2,1)} %bitcast.16, bf16[2,160,512]{2,1,0:T(8,128)(2,1)} %bitcast.17, s32[1,512]{1,0:T(1,128)S(1)} %bitcast.10, s32[1,512]{1,0:T(1,128)S(1)} %bitcast.11, ...), custom_call_target="tpu_custom_call" | custom-call | tf_op jit(solution)/shard_map/pallas_call | solution.py:555
  39.1 0.6 %multiply_add_fusion = (f32[6,4,128]{2,1,0:T(4,128)}, f32[6,4,128]{2,1,0:T(4,128)}) fusion(f32[6,4,128]{2,1,0:T(4,128)S(1)} %get-tuple-element.8, f32[6,4,128]{2,1,0:T(4,128)S(1)} %get-tuple-element.10, f32[128]{0:T(128)S(1)} %bitcast.15, f32[128]{0:T(128)S(1)} %bitcast.14, f32[128]{0:T(128)S(1)} %bitcast.13), kind=kLoop, calls=%fused_computation | loop fusion | flops 12288 | bytes 50688 | tf_op jit(solution)/shard_map/add | solution.py:594
Async XLA Ops:
  0.6 0.7 %copy-start.2 = (s32[1,1,512]{2,1,0:T(1,128)S(1)}, s32[1,1,512]{2,1,0:T(1,128)}, u32[]{:S(2)}) copy-start(s32[1,1,512]{2,1,0:T(1,128)} %param.9) | copy-start | bytes 6148
  0.6 0.7 %copy-start.1 = (s32[1,1,512]{2,1,0:T(1,128)S(1)}, s32[1,1,512]{2,1,0:T(1,128)}, u32[]{:S(2)}) copy-start(s32[1,1,512]{2,1,0:T(1,128)} %param.8) | copy-start | bytes 6148
  0.7 0.7 %copy-start = (s32[1,1,512]{2,1,0:T(1,128)S(1)}, s32[1,1,512]{2,1,0:T(1,128)}, u32[]{:S(2)}) copy-start(s32[1,1,512]{2,1,0:T(1,128)} %param.7) | copy-start | bytes 6148

commit v6 on v5

--- a/solution.py
+++ b/solution.py
@@ -231,8 +231,10 @@
         far, totals = list(carry[:20]), list(carry[20:])
         for row in range(TILE_ROWS):
             g = field[block, row]
-            here = dynamic_key(block, row)
-            for t in range(TILE_ROWS):
+            known = isinstance(block, int)
+            here = float(row_key(block, row)) if known else dynamic_key(block, row)
+            near = [t for t in range(TILE_ROWS) if not known or reach(block, row, 4, t)]
+            for t in near:
                 for i in range(5):
                     far[t * 5 + i] = jnp.where(keys[16 + t, i] == here, g, far[t * 5 + i])
             by_a, by_b = halves(moments[block, 0, row])
@@ -241,7 +243,7 @@
             for i, shift in enumerate(SHIFTS):
                 part = turn(value, shift)
                 key = keys[block * TILE_ROWS + row, i]
-                for t in range(TILE_ROWS):
+                for t in near:
                     hit = key == float(row_key(4, t))
                     totals[t] = totals[t] + jnp.where(hit, part, 0.0)
         return tuple(far) + tuple(totals)
@@ -250,14 +252,11 @@
         landed(2 * k + 1)
         return step(2 * k + 1, carry)
 
-    def corner(k, carry):
-        block = 2 * k + 2 * (k // 2)
+    carry = step(4, (jnp.zeros((8, NCOLS), F32),) * 24)
+    carry = lax.fori_loop(0, len(EDGES), edge, carry)
+    for block in CORNERS:
         landed(block)
-        return step(block, carry)
-
-    carry = step(jnp.int32(4), (jnp.zeros((8, NCOLS), F32),) * 24)
-    carry = lax.fori_loop(0, len(EDGES), edge, carry)
-    carry = lax.fori_loop(0, len(CORNERS), corner, carry)
+        carry = step(block, carry)
     out = []
     for t in range(TILE_ROWS):
         far = carry[t * 5 + 2]
@@ -277,9 +276,9 @@
     group_one,
     coords_ref,
     targets_ref,
-    first_ref,
-    second_ref,
-    count_ref,
+    first,
+    second,
+    count,
     gradient_ref,
     product_ref,
     solution_scale_ref,
@@ -287,9 +286,6 @@
     gradient_scale_ref,
     coords,
     targets,
-    first,
-    second,
-    count,
     chosen,
     table,
     terms,
@@ -328,9 +324,6 @@
         loads.append(pltpu.make_async_copy(source, target, load_sems.at[len(loads)]))
         loads[-1].start()
 
-    load(count_ref, count)
-    load(first_ref, first)
-    load(second_ref, second)
     blocks = coords_ref.shape[2] // NCOLS
     for i in range(blocks):
         lanes = pl.ds(i * NCOLS, NCOLS)
@@ -382,13 +375,11 @@
     for a, b in NEIGHBOURS:
         signal(barrier, neighbour(a, b))
 
-    for copy in loads[:3]:
-        copy.wait()
     place_table(first, chosen)
 
     def ready(i):
-        loads[3 + 2 * i].wait()
-        loads[4 + 2 * i].wait()
+        loads[2 * i].wait()
+        loads[2 * i + 1].wait()
 
     squares = pair_tables(coords, targets, first, second, count, table, ready)
 
@@ -555,14 +546,11 @@
         gradient, product, *scales = pl.pallas_call(
             functools.partial(kernel, sections, bands, group_one),
             out_shape=tuple(jax.ShapeDtypeStruct(s, F32) for s in (shape, shape) + ((1, NCOLS),) * 3),
-            in_specs=[anywhere] * 5,
+            in_specs=[anywhere] * 2 + [vmem] * 3,
             out_specs=(vmem,) * 5,
             scratch_shapes=[
                 pltpu.VMEM((4, slots, pairs), coords.dtype),
                 pltpu.VMEM((2, slots, pairs), targets.dtype),
-                pltpu.VMEM((1, pairs), jnp.int32),
-                pltpu.VMEM((1, pairs), jnp.int32),
-                pltpu.VMEM((1, pairs), jnp.int32),
                 pltpu.VMEM((TILE_ROWS, NCOLS, pairs), jnp.bfloat16),
                 pltpu.VMEM((8 * len(GROUPS), pairs), F32),
                 pltpu.VMEM((TILE_ROWS,) + tile, F32),
@@ -576,7 +564,7 @@
                 pltpu.VMEM((group_one, NCOLS), F32),
                 pltpu.VMEM((group_two, NCOLS), F32),
             ]
-            + [dma((3 + 2 * (pairs // NCOLS),))]
+            + [dma((2 * (pairs // NCOLS),))]
             + [dma((8,)), dma((9,))] * 3
             + [dma((2,))] * 2
             + [pltpu.SemaphoreType.REGULAR],

time: 39.9 us -> 39.8 us (level)
  no operation moved by 1% of the time
where the time goes in v6:
time: 39.8 us; the launch traced here: 39.6 us
  Pallas kernels  37.7 us (95%)
  local copies, waits for them, and re-layouts  0.69 us (2%)
  between operations  0.66 us (2%)
  other arithmetic  0.61 us (2%)
    pallas_call x1, Pallas kernels, on_device(): pl.pallas_call(functools.partial(kernel, sections, bands, group_one), out...  37.7 us

profile of v6, /device:TPU:1, one launch (start us, length us, event | category | flops | bytes accessed | tf_op | source)
XLA Modules:
  0.0 39.6 jit_solution(17614051241340963253)
XLA Ops:
  0.6 0.0 copy-start.2
  0.6 0.0 copy-start.1
  0.7 0.0 copy-start
  0.7 0.7 %copy-done.2 = s32[1,1,512]{2,1,0:T(1,128)S(1)} copy-done((s32[1,1,512]{2,1,0:T(1,128)S(1)}, s32[1,1,512]{2,1,0:T(1,128)}, u32[]{:S(2)}) %copy-start.2) | copy-done | bytes 2072
  1.3 0.0 copy-done.1
  1.3 0.0 copy-done
  1.3 37.7 %shard_map.68 = (f32[6,4,128]{2,1,0:T(4,128)S(1)}, f32[6,4,128]{2,1,0:T(4,128)S(1)}, f32[1,128]{1,0:T(1,128)S(1)}, f32[1,128]{1,0:T(1,128)S(1)}, f32[1,128]{1,0:T(1,128)S(1)}) custom-call(bf16[4,160,512]{2,1,0:T(8,128)(2,1)} %bitcast.16, bf16[2,160,512]{2,1,0:T(8,128)(2,1)} %bitcast.17, s32[1,512]{1,0:T(1,128)S(1)} %bitcast.10, s32[1,512]{1,0:T(1,128)S(1)} %bitcast.11, ...), custom_call_target="tpu_custom_call" | custom-call | tf_op jit(solution)/shard_map/pallas_call | solution.py:546
  39.0 0.6 %multiply_add_fusion = (f32[6,4,128]{2,1,0:T(4,128)}, f32[6,4,128]{2,1,0:T(4,128)}) fusion(f32[6,4,128]{2,1,0:T(4,128)S(1)} %get-tuple-element.8, f32[6,4,128]{2,1,0:T(4,128)S(1)} %get-tuple-element.10, f32[128]{0:T(128)S(1)} %bitcast.15, f32[128]{0:T(128)S(1)} %bitcast.14, f32[128]{0:T(128)S(1)} %bitcast.13), kind=kLoop, calls=%fused_computation | loop fusion | flops 12288 | bytes 50688 | tf_op jit(solution)/shard_map/add | solution.py:582
Async XLA Ops:
  0.6 0.7 %copy-start.2 = (s32[1,1,512]{2,1,0:T(1,128)S(1)}, s32[1,1,512]{2,1,0:T(1,128)}, u32[]{:S(2)}) copy-start(s32[1,1,512]{2,1,0:T(1,128)} %param.9) | copy-start | bytes 6148
  0.6 0.7 %copy-start.1 = (s32[1,1,512]{2,1,0:T(1,128)S(1)}, s32[1,1,512]{2,1,0:T(1,128)}, u32[]{:S(2)}) copy-start(s32[1,1,512]{2,1,0:T(1,128)} %param.8) | copy-start | bytes 6148
  0.7 0.7 %copy-start = (s32[1,1,512]{2,1,0:T(1,128)S(1)}, s32[1,1,512]{2,1,0:T(1,128)}, u32[]{:S(2)}) copy-start(s32[1,1,512]{2,1,0:T(1,128)} %param.7) | copy-start | bytes 6148
